TPU v7x, 1024 devices: a whole 8x8x8 slice. The times are simulated.
1024 devices in a mesh: gx: 128 (over y, x, core), gy: 8 (over z).
Axes of the slice: x: 8, y: 8, z: 8, core: 2. Of those that a mesh axis runs over, the one named last changes fastest.
Arguments:
- load: float32 [3, 256, 64, 128], P(None, 'gx', 'gy'), may hold values from -12 to 12
- viscous: float32 [6, 256, 64, 128], P(None, 'gx', 'gy'), may hold values from -4 to 4
- material: int32 [256, 64, 128], P('gx', 'gy'), may hold values from 0 to 15
- free_nodes: int32 [256, 64, 128], P('gx', 'gy'), may hold values 0 or 1
- moduli_table: float32 [3, 16], replicated, may hold values from 0.5 to 5
- relax_time: float32 [16], replicated, may hold values from 0.1 to 10
Outputs:
- displacement: float32 [3, 256, 64, 128], P(None, 'gx', 'gy')
- viscous_next: float32 [6, 256, 64, 128], P(None, 'gx', 'gy')
All inputs are finite; a program needn't handle non-finite values. No bound on the sum of `free_nodes` on one device may be relied on, other than what follows from the above.
Results may differ from a plain program's by a relative error of at most 0.00035.
Values sent between devices are 32-bit elements; how exact they have to be, the bound alone decides.
No kernel may reach another device: no remote copies, remote signals or barrier semaphores. Data moves between devices by JAX's collectives and lax.ppermute only.
A program may use at most 64 MiB of HBM per device.

v0:
```python
from functools import partial
import math

import jax
import jax.numpy as jnp
from jax import lax
from jax.sharding import PartitionSpec as P

ITERS = 4


GAUSS_LOW = 0.5 - 0.5 / math.sqrt(3.0)
GAUSS_POINTS = (GAUSS_LOW, 1.0 - GAUSS_LOW)
CENTROID = (0.5, 0.5, 0.5)


def passed_along(value, axis, steps):
    count = lax.axis_size(axis)
    first, last = (max(0, -steps), min(count, count - steps))
    return lax.ppermute(value, axis, [(source, source + steps) for source in range(first, last)])


def blend(field, axis, weight):
    length = field.shape[axis]
    if axis == 3:
        lower = field
        upper = jnp.concatenate([field[:, :, :, 1:], jnp.zeros_like(field[:, :, :, :1])], axis=3)
    else:
        lower = lax.slice_in_dim(field, 0, length - 1, axis=axis)
        upper = lax.slice_in_dim(field, 1, length, axis=axis)
    if weight is None:
        return upper - lower
    return (1.0 - weight) * lower + weight * upper


def point_strain(nodes, point):
    first, second, third = point
    along_x = blend(blend(blend(nodes, 1, None), 2, second), 3, third)
    along_y = blend(blend(blend(nodes, 1, first), 2, None), 3, third)
    along_z = blend(blend(blend(nodes, 1, first), 2, second), 3, None)
    return jnp.stack(
        [
            along_x[0],
            along_y[1],
            along_z[2],
            0.5 * (along_y[2] + along_z[1]),
            0.5 * (along_x[2] + along_z[0]),
            0.5 * (along_x[1] + along_y[0]),
        ]
    )


def elastic_load(strain, lame_first, shear, weight):
    trace = strain[0] + strain[1] + strain[2]
    normal_part = weight * (lame_first * trace + 2.0 * shear * strain[:3])
    shear_part = weight * 4.0 * shear * strain[3:]
    return jnp.concatenate([normal_part, shear_part], axis=0)


def arm_load(strain, shear_arm):
    return jnp.concatenate([2.0 * shear_arm * strain[:3], 4.0 * shear_arm * strain[3:]], axis=0)


def element_forces(nodes, lame_first, shear_inf, shear_arm):
    total = jnp.zeros_like(nodes)
    for first in GAUSS_POINTS:
        for second in GAUSS_POINTS:
            for third in GAUSS_POINTS:
                strain, pullback = jax.vjp(
                    partial(point_strain, point=(first, second, third)), nodes
                )
                total = total + pullback(elastic_load(strain, lame_first, shear_inf, 0.125))[0]
    strain, pullback = jax.vjp(partial(point_strain, point=CENTROID), nodes)
    return total + pullback(arm_load(strain, shear_arm))[0]


def history_forces(viscous, shear_arm, nodes_shape):
    blank = jnp.zeros(nodes_shape, viscous.dtype)
    strain, pullback = jax.vjp(partial(point_strain, point=CENTROID), blank)
    return pullback(arm_load(viscous, shear_arm))[0]


def from_below_x(layer):
    return passed_along(layer, "gx", 1)


def from_below_y(layer):
    return passed_along(layer, "gy", 1)


def from_above_x(layer):
    return passed_along(layer, "gx", -1)


def from_above_y(layer):
    return passed_along(layer, "gy", -1)


def pull_lower(field):
    wide = jnp.concatenate([from_below_x(field[:, -1:]), field], axis=1)
    return jnp.concatenate([from_below_y(wide[:, :, -1:]), wide], axis=2)


def send_back(forces):
    incoming = from_above_y(forces[:, :, :1])
    inner = forces[:, :, 1:]
    inner = jnp.concatenate([inner[:, :, :-1], inner[:, :, -1:] + incoming], axis=2)
    arriving = from_above_x(inner[:, :1])
    rest = inner[:, 1:]
    return jnp.concatenate([rest[:, :-1], rest[:, -1:] + arriving], axis=1)


def inner_sums(residual, image):
    return lax.psum((jnp.sum(residual * residual), jnp.sum(residual * image)), ("gx", "gy"))


def shards(load, viscous, material, free_nodes, moduli_table, relax_time):
    classes = relax_time.shape[0]
    picks = (material[None] == jnp.arange(classes, dtype=jnp.int32)[:, None, None, None]).astype(
        jnp.float32
    )

    def lookup(values):
        return jnp.sum(picks * values[:, None, None, None], axis=0)

    lame_first = lookup(moduli_table[0])
    shear_inf = lookup(moduli_table[1])
    retain = lookup(relax_time / (relax_time + 1.0))
    shear_arm = lookup(moduli_table[2]) * retain
    mask = free_nodes.astype(jnp.float32)
    nodes_shape = (3, load.shape[1] + 1, load.shape[2] + 1, load.shape[3])
    history = send_back(history_forces(viscous, shear_arm, nodes_shape))
    right = mask * (load + history)

    def operator(field):
        masked = mask * field
        forces = element_forces(pull_lower(masked), lame_first, shear_inf, shear_arm)
        return mask * send_back(forces) + (1.0 - mask) * field

    displacement = jnp.zeros_like(load)
    residual = right
    image = operator(residual)
    norm_now, curvature = inner_sums(residual, image)
    alpha = norm_now / curvature
    direction, along = (residual, image)
    for step in range(ITERS):
        displacement = displacement + alpha * direction
        residual = residual - alpha * along
        if step + 1 < ITERS:
            image = operator(residual)
            norm_next, curvature = inner_sums(residual, image)
            ratio = norm_next / norm_now
            alpha = norm_next / (curvature - ratio * norm_next / alpha)
            direction = residual + ratio * direction
            along = image + ratio * along
            norm_now = norm_next
    centre = point_strain(pull_lower(displacement), CENTROID)
    viscous_next = retain * viscous + (1.0 - retain) * centre
    return (displacement, viscous_next)


def solution(mesh):
    return jax.shard_map(
        shards,
        mesh=mesh,
        in_specs=(
            P(None, "gx", "gy", None),
            P(None, "gx", "gy", None),
            P("gx", "gy", None),
            P("gx", "gy", None),
            P(),
            P(),
        ),
        out_specs=(P(None, "gx", "gy", None), P(None, "gx", "gy", None)),
        check_vma=False,
    )
```

profile of v0, /device:TPU:1, one launch (start us, length us, event | category | flops | bytes accessed | tf_op | source)
XLA Modules:
  0.0 633.9 jit_solution(9858629074307869894)
XLA Ops:
  3.9 1.3 collective-permute-start
  5.3 5.4 collective-permute-done
  10.7 14.8 %collective-permute-start.1 = (f32[3,1,8,128]{3,2,1,0:T(8,128)S(1)}, f32[3,1,8,128]{3,2,1,0:T(8,128)S(1)}, u32[]{:S(2)}, u32[]{:S(2)}) collective-permute-start(f32[3,1,8,128]{3,2,1,0:T(8,128)S(1)} %get-tuple-element.729), channel_id=1, source_target_pairs={{8,0},{16,8},{24,16},{32,24},{40,32},{48,40},{56,48},{64,56},{72,6... | collective-permute-start | bytes 36872 | tf_op jit(solution)/shard_map/ppermute | solution.py:20
  26.4 1.9 collective-permute-start.2
  29.5 1.4 collective-permute-start.3
  39.1 1.3 collective-permute-start.4
  40.4 3.3 collective-permute-done.4
  43.7 4.1 collective-permute-start.5
  47.8 3.1 collective-permute-done.5
  51.6 120.1 %all-reduce.901 = (f32[]{:T(128)}, f32[]{:T(128)}) all-reduce(f32[]{:T(128)} %get-tuple-element.9, f32[]{:T(128)} %get-tuple-element.8), channel_id=1, replica_groups=mesh['gx'=128,'gy'=8] {'gx','gy'}, use_global_device_ids=true, to_apply=%region_3.0 | all-reduce | flops 2 | bytes 16 | tf_op jit(solution)/shard_map/psum | solution.py:114
  173.1 4.0 collective-permute-start.6
  189.2 1.3 collective-permute-start.8
  190.5 3.3 collective-permute-done.8
  193.8 4.1 collective-permute-start.9
  197.9 3.2 collective-permute-done.9
  201.8 117.2 %all-reduce.900 = (f32[]{:T(128)}, f32[]{:T(128)}) all-reduce(f32[]{:T(128)} %get-tuple-element.3, f32[]{:T(128)} %get-tuple-element.2), channel_id=1, replica_groups=mesh['gx'=128,'gy'=8] {'gx','gy'}, use_global_device_ids=true, to_apply=%region_9.0 | all-reduce | flops 2 | bytes 16 | tf_op jit(solution)/shard_map/psum | solution.py:114
  323.5 2.4 collective-permute-start.10
  326.9 3.8 collective-permute-start.11
  340.7 1.3 collective-permute-start.12
  342.0 3.6 collective-permute-done.12
  345.7 2.3 collective-permute-start.13
  348.0 4.9 collective-permute-done.13
  353.6 116.8 %all-reduce.899 = (f32[]{:T(128)}, f32[]{:T(128)}) all-reduce(f32[]{:T(128)} %get-tuple-element.7, f32[]{:T(128)} %get-tuple-element.6), channel_id=1, replica_groups=mesh['gx'=128,'gy'=8] {'gx','gy'}, use_global_device_ids=true, to_apply=%region_13.0 | all-reduce | flops 2 | bytes 16 | tf_op jit(solution)/shard_map/psum | solution.py:114
  474.2 3.9 collective-permute-start.14
  478.9 2.4 collective-permute-start.15
  490.1 1.3 collective-permute-start.16
  491.4 3.3 collective-permute-done.16
  494.7 4.1 collective-permute-start.17
  498.8 3.4 collective-permute-done.17
  502.8 118.1 %all-reduce.898 = (f32[]{:T(128)}, f32[]{:T(128)}) all-reduce(f32[]{:T(128)} %get-tuple-element.5, f32[]{:T(128)} %get-tuple-element.4), channel_id=1, replica_groups=mesh['gx'=128,'gy'=8] {'gx','gy'}, use_global_device_ids=true, to_apply=%region_17.0 | all-reduce | flops 2 | bytes 16 | tf_op jit(solution)/shard_map/psum | solution.py:114
  624.9 2.3 collective-permute-start.18
  628.3 3.8 collective-permute-start.19
  (712 shorter events, 48.5 us)
Async XLA Ops:
  0.6 1.5 copy-start.19
  2.1 0.8 copy-start.2
  3.9 6.7 %collective-permute-start = (f32[3,3,1,128]{3,2,1,0:T(1,128)S(1)}, f32[3,3,1,128]{3,2,1,0:T(1,128)S(1)}, u32[]{:S(2)}, u32[]{:S(2)}) collective-permute-start(f32[3,3,1,128]{3,2,1,0:T(1,128)S(1)} %pad_add_fusion.272), channel_id=1, source_target_pairs={{1,0},{2,1},{3,2},{4,3},{5,4},{6,5},{7,6},{9,8},{10,9},{11,10},{12... | collective-permute-start | bytes 13832 | tf_op jit(solution)/shard_map/ppermute | solution.py:20
  10.7 14.9 %copy-start.17 = (s32[2,8,128]{2,1,0:T(8,128)S(1)}, s32[2,8,128]{2,1,0:T(8,128)}, u32[]{:S(2)}) copy-start(s32[2,8,128]{2,1,0:T(8,128)} %param.9) | copy-start | bytes 24580
  10.7 15.7 %collective-permute-start.1 = (f32[3,1,8,128]{3,2,1,0:T(8,128)S(1)}, f32[3,1,8,128]{3,2,1,0:T(8,128)S(1)}, u32[]{:S(2)}, u32[]{:S(2)}) collective-permute-start(f32[3,1,8,128]{3,2,1,0:T(8,128)S(1)} %get-tuple-element.729), channel_id=1, source_target_pairs={{8,0},{16,8},{24,16},{32,24},{40,32},{48,40},{56,48},{64,56},{72,6... | collective-permute-start | bytes 36872 | tf_op jit(solution)/shard_map/ppermute | solution.py:20
  25.6 0.8 copy-start.18
  26.4 3.1 collective-permute-start.2
  29.5 2.1 collective-permute-start.3
  34.2 0.7 slice-start.1
  35.2 0.7 slice-start.5
  36.5 0.7 slice-start
  39.1 4.6 collective-permute-start.4
  43.7 7.3 %collective-permute-start.5 = (f32[3,1,8,128]{3,2,1,0:T(8,128)S(1)}, f32[3,1,8,128]{3,2,1,0:T(8,128)S(1)}, u32[]{:S(2)}, u32[]{:S(2)}) collective-permute-start(f32[3,1,8,128]{3,2,1,0:T(8,128)S(1)} %get-tuple-element.727), channel_id=1, source_target_pairs={{8,0},{16,8},{24,16},{32,24},{40,32},{48,40},{56,48},{64,56},{72,6... | collective-permute-start | bytes 36872 | tf_op jit(solution)/shard_map/ppermute | solution.py:20
  173.1 4.9 collective-permute-start.6
  177.9 2.0 collective-permute-start.7
  183.6 0.7 slice-start.12
  186.6 0.7 slice-start.7
  189.2 4.6 collective-permute-start.8
  193.8 7.3 %collective-permute-start.9 = (f32[3,1,8,128]{3,2,1,0:T(8,128)S(1)}, f32[3,1,8,128]{3,2,1,0:T(8,128)S(1)}, u32[]{:S(2)}, u32[]{:S(2)}) collective-permute-start(f32[3,1,8,128]{3,2,1,0:T(8,128)S(1)} %get-tuple-element.725), channel_id=1, source_target_pairs={{8,0},{16,8},{24,16},{32,24},{40,32},{48,40},{56,48},{64,56},{72,6... | collective-permute-start | bytes 36872 | tf_op jit(solution)/shard_map/ppermute | solution.py:20
  323.5 3.5 collective-permute-start.10
  326.9 4.5 collective-permute-start.11
  335.1 0.7 slice-start.13
  340.7 4.9 collective-permute-start.12
  345.7 7.3 %collective-permute-start.13 = (f32[3,1,8,128]{3,2,1,0:T(8,128)S(1)}, f32[3,1,8,128]{3,2,1,0:T(8,128)S(1)}, u32[]{:S(2)}, u32[]{:S(2)}) collective-permute-start(f32[3,1,8,128]{3,2,1,0:T(8,128)S(1)} %get-tuple-element.723), channel_id=1, source_target_pairs={{8,0},{16,8},{24,16},{32,24},{40,32},{48,40},{56,48},{64,56},{72,6... | collective-permute-start | bytes 36872 | tf_op jit(solution)/shard_map/ppermute | solution.py:20
  474.2 4.7 collective-permute-start.14
  478.9 3.2 collective-permute-start.15
  485.5 0.7 slice-start.4
  490.1 4.6 collective-permute-start.16
  494.7 7.5 %collective-permute-start.17 = (f32[3,1,8,128]{3,2,1,0:T(8,128)S(1)}, f32[3,1,8,128]{3,2,1,0:T(8,128)S(1)}, u32[]{:S(2)}, u32[]{:S(2)}) collective-permute-start(f32[3,1,8,128]{3,2,1,0:T(8,128)S(1)} %get-tuple-element.721), channel_id=1, source_target_pairs={{8,0},{16,8},{24,16},{32,24},{40,32},{48,40},{56,48},{64,56},{72,6... | collective-permute-start | bytes 36872 | tf_op jit(solution)/shard_map/ppermute | solution.py:20
  624.9 7.9 %copy-start = (f32[3,2,8,128]{3,2,1,0:T(8,128)}, f32[3,2,8,128]{3,2,1,0:T(8,128)S(1)}, u32[]{:S(2)}) copy-start(f32[3,2,8,128]{3,2,1,0:T(8,128)S(1)} %multiply_add_fusion.10) | copy-start | bytes 73732
  624.9 3.4 collective-permute-start.18
  628.3 4.5 collective-permute-start.19
  (22 other events, 14.1 us)
where the time goes:
time: 639 us; the launch traced here: 634 us
  blocking collectives  472 us (74%)
  starting transfers between devices  63.1 us (10%)
  waiting for transfers between devices  42.9 us (7%)
  local copies, waits for them, and re-layouts  21.1 us (3%)
  between operations  17.9 us (3%)
  other arithmetic  16.7 us (3%)
    psum x4, blocking collectives, inner_sums(): lax.psum((jnp.sum(residual * residual), jnp.sum(residual * image)), ('gx'...  472 us
    ppermute x20, starting transfers between devices, passed_along(): lax.ppermute(value, axis, [(source, source + steps) for source in range(f...  63.1 us
    ppermute x20, waiting for transfers between devices, passed_along(): lax.ppermute(value, axis, [(source, source + steps) for source in range(f...  42.9 us
  transfers between devices with their start and end apart: 20, of which 20 were waited for; matrix products, arithmetic and copies ran while one was open for 0% of the time, Pallas kernels for 0%

commit v1 on v0

v1 whole, which is shorter than its diff:
```python
import math

import jax
import jax.numpy as jnp
from jax import lax
from jax.experimental import pallas as pl
from jax.experimental.pallas import tpu as pltpu
from jax.sharding import Mesh, PartitionSpec as P

ITERS = 4
ROWS = 16
LAYERS = 10
FIELDS = 11
CLASSES = 16
TINY_PIVOT = 1e-6

F32 = jnp.float32
SDS = jax.ShapeDtypeStruct
VMEM = pl.BlockSpec(memory_space=pltpu.VMEM)
SMEM = pl.BlockSpec(memory_space=pltpu.SMEM)
PAIRS = ("ss", "sd", "ds", "dd")


def call(body, out_shape, n_in, scratch=(), first_scalar=False, flops=100000):
    specs = [VMEM] * n_in
    if first_scalar:
        specs[0] = SMEM
    many = isinstance(out_shape, (list, tuple))
    return pl.pallas_call(
        body,
        out_shape=out_shape,
        in_specs=specs,
        out_specs=[VMEM] * len(out_shape) if many else VMEM,
        scratch_shapes=list(scratch),
        compiler_params=pltpu.CompilerParams(vmem_limit_bytes=24 * 1024 * 1024),
        cost_estimate=pl.CostEstimate(flops=flops, bytes_accessed=100000, transcendentals=0),
    )


def pack_body(load, viscous, material, free, moduli, relax, own, low, high, table):
    for field in range(FIELDS):
        layers = []
        for layer in range(2):
            if field < 3:
                tile = load[field, layer]
            elif field < 9:
                tile = viscous[field - 3, layer]
            elif field == 9:
                tile = material[layer].astype(F32) - float(CLASSES)
            else:
                tile = free[layer].astype(F32)
            own[2 * field + layer] = tile
            layers.append(tile)
        row = lax.broadcasted_iota(jnp.int32, (8, 128), 0)
        low[field] = jnp.where(row < 4, layers[0], pltpu.roll(layers[1], 4, 0))
        high[field] = jnp.where(row < 4, pltpu.roll(layers[0], 4, 0), layers[1])
    time = relax[...]
    retain = time / (time + 1.0)
    arm = moduli[2:3] * retain
    bound = jnp.max(moduli[0:1] + 2.0 * (moduli[1:2] + arm), axis=1, keepdims=True)
    table[...] = jnp.zeros((8, 128), F32)
    table[0:1, 0:CLASSES] = moduli[0:1] * (1.0 / 16.0)
    table[1:2, 0:CLASSES] = moduli[1:2] * (1.0 / 16.0)
    table[2:3, 0:CLASSES] = arm * (1.0 / 16.0)
    table[3:4, 0:CLASSES] = retain
    table[4:5] = jnp.broadcast_to(1.0 / bound, (1, 128))


def widen_body(own, above, below, wide):
    row = lax.broadcasted_iota(jnp.int32, (8, 128), 0)
    for field in range(FIELDS):
        upper, lower = above[field], below[field]
        uppers = (upper, pltpu.roll(upper, 4, 0))
        lowers = (pltpu.roll(lower, 4, 0), lower)
        for layer in range(2):
            k = 2 * field + layer
            wide[k, 0:8] = own[k]
            wide[k, 8:16] = jnp.where(row < 4, uppers[layer], lowers[layer])


def choose_body(core, wide, left, right, out):
    @pl.when(core[0] == 0)
    def _():
        out[0] = wide[...]
        out[1] = right[...]

    @pl.when(core[0] != 0)
    def _():
        out[0] = left[...]
        out[1] = wide[...]


def iota(axis, shape=(ROWS, 128)):
    return lax.broadcasted_iota(jnp.int32, shape, axis)


def next_lane(tile):
    return jnp.where(iota(1) < 127, pltpu.roll(tile, 127, 1), 0.0)


def previous_lane(tile):
    return jnp.where(iota(1) > 0, pltpu.roll(tile, 1, 1), 0.0)


def node_pairs(tile, last=True):
    lower = pltpu.roll(tile, 1, 0)
    parts = {}
    for name, part in (("s", tile + lower), ("d", tile - lower)):
        upper = next_lane(part)
        parts[name + "s"] = part + upper
        if last or name == "s":
            parts[name + "d"] = upper - part
    return parts


def element_modes(lower, upper):
    modes = []
    for below, above in zip(lower, upper):
        mode = {"d" + pair: above[pair] - below[pair] for pair in above}
        mode.update({"s" + pair: above[pair] + below[pair] for pair in above if pair != "ss"})
        modes.append(mode)
    return modes


def element_loads(modes, moduli):
    lame, both, lame_third, shear_third, cubic = moduli
    u, v, w = modes
    fu, fv, fw = {}, {}, {}
    trace = lame * (u["dss"] + v["sds"] + w["ssd"])
    twice = both + both
    fu["dss"] = trace + twice * u["dss"]
    fv["sds"] = trace + twice * v["sds"]
    fw["ssd"] = trace + twice * w["ssd"]
    fw["sds"] = fv["ssd"] = both * (w["sds"] + v["ssd"])
    fw["dss"] = fu["ssd"] = both * (w["dss"] + u["ssd"])
    fv["dss"] = fu["sds"] = both * (v["dss"] + u["sds"])
    triple = 3.0 * shear_third
    part = lame_third * (u["dds"] + w["sdd"])
    fu["dds"] = part + triple * u["dds"]
    fw["sdd"] = part + triple * w["sdd"]
    part = lame_third * (v["dds"] + w["dsd"])
    fv["dds"] = part + triple * v["dds"]
    fw["dsd"] = part + triple * w["dsd"]
    part = lame_third * (u["dsd"] + v["sdd"])
    fu["dsd"] = part + triple * u["dsd"]
    fv["sdd"] = part + triple * v["sdd"]
    part = w["dds"] + v["dsd"] + u["sdd"]
    fw["dds"] = shear_third * (part + w["dds"])
    fv["dsd"] = shear_third * (part + v["dsd"])
    fu["sdd"] = shear_third * (part + u["sdd"])
    for mode, force in zip(modes, (fu, fv, fw)):
        force["ddd"] = cubic * mode["ddd"]
    return fu, fv, fw


def plus(a, b):
    return b if a is None else a if b is None else a + b


def to_nodes(forces):
    uppers, lowers = [], []
    for force in forces:
        upper, lower = {}, {}
        for pair in PAIRS:
            s, d = force.get("s" + pair), force.get("d" + pair)
            upper[pair] = plus(s, d)
            lower[pair] = None if s is None and d is None else (-d if s is None else s if d is None else s - d)
        uppers.append(upper)
        lowers.append(lower)
    return uppers, lowers


def node_force(pairs):
    along = {}
    for name in "sd":
        s, d = pairs[name + "s"], pairs[name + "d"]
        if d is None:
            along[name] = s + previous_lane(s)
        else:
            along[name] = (s - d) + previous_lane(s + d)
    return (along["s"] + along["d"]) + pltpu.roll(along["s"] - along["d"], ROWS - 1, 0)


def merged(first, second):
    return [{pair: plus(a[pair], b[pair]) for pair in PAIRS} for a, b in zip(first, second)]


def pick(table, row, index):
    entries = jnp.broadcast_to(table[row : row + 1], (ROWS, 128))
    return jnp.take_along_axis(entries, index, axis=1, mode="promise_in_bounds")


def krylov_body(left, rec, wide, right, table, basis, sums, vec, mask, moduli, images):
    blocks = (left, rec.at[0], wide, rec.at[1], right)

    def field(number, layer):
        return blocks[layer // 2][2 * number + layer % 2]

    pending = None
    for layer in range(LAYERS):
        index = field(9, layer).astype(jnp.int32) + CLASSES
        lame, shear, arm = (pick(table, row, index) for row in range(3))
        moduli[0, layer] = lame
        moduli[1, layer] = shear + arm
        moduli[2, layer] = lame * (1.0 / 3.0)
        moduli[3, layer] = shear * (1.0 / 3.0)
        moduli[4, layer] = (lame + 4.0 * shear) * (1.0 / 9.0)
        mask[layer] = field(10, layer)
        factor = 8.0 * arm
        xx, yy, zz, yz, xz, xy = (factor * field(3 + part, layer) for part in range(6))
        forces = (
            {"dss": xx, "ssd": xz, "sds": xy},
            {"sds": yy, "ssd": yz, "dss": xy},
            {"ssd": zz, "sds": yz, "dss": xz},
        )
        upper, lower = to_nodes(forces)
        if pending is not None:
            node = layer - 1
            for comp, pairs in enumerate(merged(pending, lower)):
                vec[0, comp, node] = mask[node] * (field(comp, node) + node_force(pairs))
        pending = upper

    scale = jnp.broadcast_to(table[4:5], (ROWS, 128))

    def masked_pairs(step, layer):
        return [node_pairs(mask[layer] * vec[step, comp, layer]) for comp in range(3)]

    for step in range(ITERS - 1):
        below = masked_pairs(step, step)
        pending = None
        for layer in range(step + 1, LAYERS - 1 - step):
            above = masked_pairs(step, layer)
            loads = element_loads(element_modes(below, above), [moduli[k, layer] for k in range(5)])
            upper, lower = to_nodes(loads)
            if pending is not None:
                node = layer - 1
                free = mask[node]
                for comp, pairs in enumerate(merged(pending, lower)):
                    value = vec[step, comp, node]
                    image = free * node_force(pairs) + (1.0 - free) * value
                    if node in (4, 5):
                        images[step, comp, node - 4] = image[0:8]
                    if step == 0:
                        fresh = scale * image - value
                    else:
                        fresh = 2.0 * (scale * image - value) - vec[step - 1, comp, node]
                    vec[step + 1, comp, node] = fresh
            pending = upper
            below = above

    last = ITERS - 1
    energy = jnp.zeros((8, 128), F32)
    below = masked_pairs(last, 3)
    for layer in (4, 5):
        above = masked_pairs(last, layer)
        modes = element_modes(below, above)
        loads = element_loads(modes, [moduli[k, layer] for k in range(5)])
        total = None
        for mode, force in zip(modes, loads):
            for name in force:
                total = plus(total, (mode[name] * force[name])[0:8])
        energy = energy + total
        for comp in range(3):
            value = vec[last, comp, layer, 0:8]
            energy = energy + (1.0 - mask[layer, 0:8]) * value * value
        below = above

    def product(first, second):
        total = None
        for comp in range(3):
            for layer in range(2):
                total = plus(total, first(comp, layer) * second(comp, layer))
        return total

    def vector(step):
        return lambda comp, layer: vec[step, comp, 4 + layer, 0:8]

    def image(step):
        return lambda comp, layer: images[step, comp, layer]

    products = []
    for i in range(ITERS):
        for j in range(i + 1):
            if i == last and j == last:
                products.append(energy)
            elif i == last:
                products.append(product(vector(i), image(j)))
            else:
                products.append(product(vector(j), image(i)))
    for i in range(ITERS):
        products.append(product(vector(0), vector(i)))
    rows = jnp.zeros((ROWS, 128), F32)
    for number, value in enumerate(products):
        rows = jnp.where(iota(0) == number, jnp.sum(value, axis=0, keepdims=True), rows)
    column = jnp.sum(rows, axis=1, keepdims=True)
    line = jnp.sum(jnp.where(iota(0) == iota(1), column, 0.0), axis=0, keepdims=True)
    sums[...] = jnp.broadcast_to(line, sums.shape)
    for step in range(ITERS):
        for comp in range(3):
            for layer in range(3):
                basis[step, comp, layer] = vec[step, comp, 3 + layer]


def final_body(sums, basis, own, table, displacement, viscous_next):
    line = jnp.sum(sums[...], axis=0, keepdims=True)
    lane = iota(1, (1, 128))

    def entry(number):
        return jnp.sum(jnp.where(lane == number, line, 0.0), axis=1, keepdims=True)

    matrix = [[entry(i * (i + 1) // 2 + j) for j in range(i + 1)] for i in range(ITERS)]
    value = [entry(10 + i) for i in range(ITERS)]
    first = [matrix[i][i] for i in range(ITERS)]
    ratio = {}
    inverse = []
    for k in range(ITERS):
        pivot = matrix[k][k]
        inverse.append(jnp.where(pivot > TINY_PIVOT * first[k], 1.0 / pivot, 0.0))
        for i in range(k + 1, ITERS):
            ratio[i, k] = matrix[i][k] * inverse[k]
            for j in range(k + 1, i + 1):
                matrix[i][j] = matrix[i][j] - ratio[i, k] * matrix[j][k]
            value[i] = value[i] - ratio[i, k] * value[k]
    value = [value[k] * inverse[k] for k in range(ITERS)]
    for k in reversed(range(ITERS)):
        for i in range(k):
            value[i] = value[i] - ratio[k, i] * value[k]
    weights = [jnp.broadcast_to(v, (ROWS, 128)) for v in value]

    pairs = []
    for layer in range(3):
        fields = []
        for comp in range(3):
            total = weights[0] * basis[0, comp, layer]
            for step in range(1, ITERS):
                total = total + weights[step] * basis[step, comp, layer]
            if layer > 0:
                displacement[comp, layer - 1] = total[0:8]
            fields.append(node_pairs(total, last=False))
        pairs.append(fields)
    for layer in range(2):
        u, v, w = element_modes(pairs[layer], pairs[layer + 1])
        strain = (
            0.25 * u["dss"],
            0.25 * v["sds"],
            0.25 * w["ssd"],
            0.125 * (w["sds"] + v["ssd"]),
            0.125 * (w["dss"] + u["ssd"]),
            0.125 * (v["dss"] + u["sds"]),
        )
        index = own[18 + layer].astype(jnp.int32) + CLASSES
        entries = jnp.broadcast_to(table[3:4], (8, 128))
        retain = jnp.take_along_axis(entries, index, axis=1, mode="promise_in_bounds")
        for part in range(6):
            old = own[6 + 2 * part + layer]
            viscous_next[part, layer] = retain * old + (1.0 - retain) * strain[part][0:8]


def shifted(value, axes, count, steps):
    pairs = [(i, i + steps) for i in range(count) if 0 <= i + steps < count]
    return lax.ppermute(value, axes, pairs)


def summed(value, axes):
    return jnp.sum(lax.all_to_all(value, axes, 0, 0), axis=0)


def solution(mesh):
    count_x, count_z = mesh.shape["gx"], mesh.shape["gy"]
    along = min(8, count_x // 2)
    across = count_x // (2 * along)
    grid = Mesh(mesh.devices.reshape(across, along, 2, count_z), ("y", "x", "core", "z"))
    chips = along * across

    def shards(load, viscous, material, free_nodes, moduli_table, relax_time):
        own, low, high, table = call(
            pack_body,
            (SDS((22, 8, 128), F32), SDS((11, 8, 128), F32), SDS((11, 8, 128), F32), SDS((8, 128), F32)),
            6,
        )(load, viscous, material, free_nodes, moduli_table, relax_time.reshape(1, -1))
        below = shifted(high, ("z",), count_z, 1)
        above = shifted(low, ("z",), count_z, -1)
        wide = call(widen_body, SDS((22, ROWS, 128), F32), 3)(own, above, below)
        left = shifted(wide, ("y", "x"), chips, 1)
        right = shifted(wide, ("y", "x"), chips, -1)
        core = lax.axis_index("core").astype(jnp.int32).reshape(1)
        given = call(choose_body, SDS((2, 22, ROWS, 128), F32), 4, first_scalar=True)(core, wide, left, right)
        taken = lax.ppermute(given, ("core",), [(0, 1), (1, 0)])
        near, far = 2 * along, across * count_z
        basis, sums = call(
            krylov_body,
            (SDS((ITERS, 3, 3, ROWS, 128), F32), SDS((near, 128), F32)),
            5,
            scratch=(
                pltpu.VMEM((ITERS, 3, LAYERS, ROWS, 128), F32),
                pltpu.VMEM((LAYERS, ROWS, 128), F32),
                pltpu.VMEM((5, LAYERS, ROWS, 128), F32),
                pltpu.VMEM((ITERS - 1, 3, 2, 8, 128), F32),
            ),
            flops=20000000,
        )(left, taken, wide, right, table)
        partial = summed(sums.reshape(near, 1, 128), ("x", "core"))
        everything = lax.all_to_all(jnp.broadcast_to(partial[None], (far, 1, 128)), ("y", "z"), 0, 0)
        return tuple(
            call(final_body, (SDS((3, 2, 8, 128), F32), SDS((6, 2, 8, 128), F32)), 4)(
                everything.reshape(far, 128), basis, own, table
            )
        )

    return jax.shard_map(
        shards,
        mesh=grid,
        in_specs=(
            P(None, ("y", "x", "core"), "z", None),
            P(None, ("y", "x", "core"), "z", None),
            P(("y", "x", "core"), "z", None),
            P(("y", "x", "core"), "z", None),
            P(),
            P(),
        ),
        out_specs=(P(None, ("y", "x", "core"), "z", None), P(None, ("y", "x", "core"), "z", None)),
        check_vma=False,
    )
```

time: 639 us -> 79.6 us (0.12)
  blocking collectives: 472 us -> 37.3 us
  waiting for transfers between devices: 42.9 us -> 4.8 us
  starting transfers between devices: 63.1 us -> 28.9 us
  between operations: 17.9 us -> 0.71 us
  local copies, waits for them, and re-layouts: 21.1 us -> 4.28 us
  other arithmetic: 16.7 us -> 0.03 us
    psum x4 -> x0, blocking collectives: 472 us -> none  [inner_sums(): lax.psum((jnp.sum(residual * residual), jnp.sum(residual * image)), ('gx'...]
    ppermute x20 -> x5, waiting for transfers between devices: 42.9 us -> 4.8 us  [the longest x4 3.52 us: shifted(): return lax.ppermute(value, axes, pairs)]
    all_to_all x0 -> x2, blocking collectives: none -> 37.3 us  [the longest x1 26.4 us: shards(): lax.all_to_all(jnp.broadcast_to(partial[None], (far, 1, 128)), ('y', 'z')...]
    ppermute x20 -> x5, starting transfers between devices: 63.1 us -> 28.9 us  [the longest x1 16 us: shards(): taken = lax.ppermute(given, ('core',), [(0, 1), (1, 0)])]
    slice x118 -> x0, local copies, waits for them, and re-layouts: 12.9 us -> none  [the longest x30 9.72 us: point_strain(): along_z[2]]
    mul x268 -> x0, other arithmetic: 7.7 us -> none  [the longest x213 7.3 us: blend(): return (1.0 - weight) * lower + weight * upper]
  transfers between devices with their start and end apart: 20 -> 5, of which waited for: 20 -> 4; matrix products, arithmetic and copies ran while one was open for 0% -> 0% of each run, Pallas kernels for 0% -> 0%
where the time goes in v1:
time: 79.6 us; the launch traced here: 79.1 us
  blocking collectives  37.3 us (47%)
  starting transfers between devices  28.9 us (36%)
  waiting for transfers between devices  4.8 us (6%)
  local copies, waits for them, and re-layouts  4.28 us (5%)
  Pallas kernels  3.04 us (4%)
    all_to_all x1, blocking collectives, shards(): lax.all_to_all(jnp.broadcast_to(partial[None], (far, 1, 128)), ('y', 'z')...  26.4 us
    ppermute x1, starting transfers between devices, shards(): taken = lax.ppermute(given, ('core',), [(0, 1), (1, 0)])  16 us
    ppermute x4, starting transfers between devices, shifted(): return lax.ppermute(value, axes, pairs)  12.9 us
    all_to_all x1, blocking collectives, summed(): return jnp.sum(lax.all_to_all(value, axes, 0, 0), axis=0)  10.9 us
    unnamed x12, local copies, waits for them, and re-layouts  4.26 us
    ppermute x4, waiting for transfers between devices, shifted(): return lax.ppermute(value, axes, pairs)  3.52 us
    pallas_call x1, Pallas kernels, shards(): call(krylov_body, (SDS((ITERS, 3, 3, ROWS, 128), F32), SDS((near, 128), F...  2.03 us
  transfers between devices with their start and end apart: 5, of which 4 were waited for; matrix products, arithmetic and copies ran while one was open for 0% of the time, Pallas kernels for 0%

profile of v1, /device:TPU:1, one launch (start us, length us, event | category | flops | bytes accessed | tf_op | source)
XLA Modules:
  0.0 79.1 jit_solution(10626825404925728568)
XLA Ops:
  0.6 0.0 copy-start.5
  0.6 0.6 copy-done.5
  1.3 0.0 copy-start
  1.3 0.8 %copy-done = f32[6,2,8,128]{3,2,1,0:T(8,128)S(1)} copy-done((f32[6,2,8,128]{3,2,1,0:T(8,128)S(1)}, f32[6,2,8,128]{3,2,1,0:T(8,128)}, u32[]{:S(2)}) %copy-start) | copy-done | bytes 49176
  2.1 0.0 copy-start.1
  2.1 0.7 copy-done.1
  2.8 0.0 copy-start.2
  2.8 0.7 copy-done.2
  3.5 0.0 copy-start.3
  3.5 0.7 copy-done.3
  4.2 0.0 copy-start.4
  4.2 0.7 copy-done.4
  4.9 0.1 shard_map.77
  5.0 1.3 %collective-permute-start = (f32[11,8,128]{2,1,0:T(8,128)S(1)}, f32[11,8,128]{2,1,0:T(8,128)S(1)}, u32[]{:S(2)}, u32[]{:S(2)}) collective-permute-start(f32[11,8,128]{2,1,0:T(8,128)S(1)} %get-tuple-element.9), channel_id=1, source_target_pairs={{1,0},{2,1},{3,2},{4,3},{5,4},{6,5},{7,6},{9,8},{10,9},{11,10},{12... | collective-permute-start | bytes 135176 | tf_op jit(solution)/shard_map/ppermute | solution.py:361
  6.3 6.4 %collective-permute-start.1 = (f32[11,8,128]{2,1,0:T(8,128)S(1)}, f32[11,8,128]{2,1,0:T(8,128)S(1)}, u32[]{:S(2)}, u32[]{:S(2)}) collective-permute-start(f32[11,8,128]{2,1,0:T(8,128)S(1)} %get-tuple-element.10), channel_id=1, source_target_pairs={{0,1},{1,2},{2,3},{3,4},{4,5},{5,6},{6,7},{8,9},{9,10},{10,11},{11... | collective-permute-start | bytes 135176 | tf_op jit(solution)/shard_map/ppermute | solution.py:361
  12.7 0.0 collective-permute-done.above
  12.7 1.1 %collective-permute-done.1.below = f32[11,8,128]{2,1,0:T(8,128)S(1)} collective-permute-done((f32[11,8,128]{2,1,0:T(8,128)S(1)}, f32[11,8,128]{2,1,0:T(8,128)S(1)}, u32[]{:S(2)}, u32[]{:S(2)}) %collective-permute-start.1) | collective-permute-done | bytes 45088 | tf_op jit(solution)/shard_map/ppermute | solution.py:361
  13.8 1.3 %collective-permute-start.3 = (f32[22,16,128]{2,1,0:T(8,128)S(1)}, f32[22,16,128]{2,1,0:T(8,128)S(1)}, u32[]{:S(2)}, u32[]{:S(2)}) collective-permute-start(f32[22,16,128]{2,1,0:T(8,128)S(1)} %shard_map.78.wide), channel_id=1, source_target_pairs={{16,0},{32,16},{48,32},{64,48},{80,64},{96,80},{112,96},{128,112},... | collective-permute-start | bytes 540680 | tf_op jit(solution)/shard_map/ppermute | solution.py:361
  15.1 4.0 %collective-permute-start.2 = (f32[22,16,128]{2,1,0:T(8,128)S(1)}, f32[22,16,128]{2,1,0:T(8,128)S(1)}, u32[]{:S(2)}, u32[]{:S(2)}) collective-permute-start(f32[22,16,128]{2,1,0:T(8,128)S(1)} %shard_map.78.wide), channel_id=1, source_target_pairs={{0,16},{16,32},{32,48},{48,64},{64,80},{80,96},{96,112},{112,128},... | collective-permute-start | bytes 540680 | tf_op jit(solution)/shard_map/ppermute | solution.py:361
  19.1 0.9 %collective-permute-done.3.right = f32[22,16,128]{2,1,0:T(8,128)S(1)} collective-permute-done((f32[22,16,128]{2,1,0:T(8,128)S(1)}, f32[22,16,128]{2,1,0:T(8,128)S(1)}, u32[]{:S(2)}, u32[]{:S(2)}) %collective-permute-start.3) | collective-permute-done | bytes 180256 | tf_op jit(solution)/shard_map/ppermute | solution.py:361
  20.0 1.5 %collective-permute-done.2.left = f32[22,16,128]{2,1,0:T(8,128)S(1)} collective-permute-done((f32[22,16,128]{2,1,0:T(8,128)S(1)}, f32[22,16,128]{2,1,0:T(8,128)S(1)}, u32[]{:S(2)}, u32[]{:S(2)}) %collective-permute-start.2) | collective-permute-done | bytes 180256 | tf_op jit(solution)/shard_map/ppermute | solution.py:361
  21.5 16.0 %collective-permute-start.4 = (f32[2,22,16,128]{3,2,1,0:T(8,128)S(1)}, f32[2,22,16,128]{3,2,1,0:T(8,128)S(1)}, u32[]{:S(2)}, u32[]{:S(2)}) collective-permute-start(f32[2,22,16,128]{3,2,1,0:T(8,128)S(1)} %shard_map.79), channel_id=1, source_target_pairs={{0,8},{8,0},{1,9},{9,1},{2,10},{10,2},{3,11},{11,3},{4,12},{12,4},... | collective-permute-start | bytes 1081352 | tf_op jit(solution)/shard_map/ppermute | solution.py:388
  37.5 1.3 %collective-permute-done.4.rec = f32[2,22,16,128]{3,2,1,0:T(8,128)S(1)} collective-permute-done((f32[2,22,16,128]{3,2,1,0:T(8,128)S(1)}, f32[2,22,16,128]{3,2,1,0:T(8,128)S(1)}, u32[]{:S(2)}, u32[]{:S(2)}) %collective-permute-start.4) | collective-permute-done | bytes 360480 | tf_op jit(solution)/shard_map/ppermute | solution.py:388
  38.8 2.0 %shard_map.80 = (f32[4,3,3,16,128]{4,3,2,1,0:T(8,128)S(1)}, f32[16,128]{1,0:T(8,128)S(1)}) custom-call(f32[22,16,128]{2,1,0:T(8,128)S(1)} %collective-permute-done.2.left, f32[2,22,16,128]{3,2,1,0:T(8,128)S(1)} %collective-permute-done.4.rec, f32[22,16,128]{2,1,0:T(8,128)S(1)} %shard_map.78.wide, f32[22,16,128]{2,1,0:T(8,128)S(1)} %collective-permute-done.3.right, ...), custom_call_target="tpu_custom_call" | custom-call | flops 20000000 | bytes 100000 | tf_op jit(solution)/shard_map/pallas_call | solution.py:390
  40.8 10.9 %all_to_all.10 = f32[16,1,128]{2,1,0:T(1,128)S(1)} all-to-all(f32[16,1,128]{2,1,0:T(1,128)S(1)} %bitcast.7), channel_id=1, replica_groups=mesh['y'=8,'x'=8,'core'=2,'z'=8] {'x','core'}, dimensions={0} | all-to-all | bytes 16384 | tf_op jit(solution)/shard_map/all_to_all | solution.py:365
  51.8 26.4 %all_to_all.11 = f32[64,1,128]{2,1,0:T(1,128)S(1)} all-to-all(f32[64,1,128]{2,1,0:T(1,128)S(1)} %broadcast_in_dim.2), channel_id=1, replica_groups=mesh['y'=8,'x'=8,'core'=2,'z'=8] {'y','z'}, dimensions={0} | all-to-all | bytes 65536 | tf_op jit(solution)/shard_map/all_to_all | solution.py:403
  78.2 0.9 %shard_map.81 = (f32[3,2,8,128]{3,2,1,0:T(8,128)}, f32[6,2,8,128]{3,2,1,0:T(8,128)}) custom-call(f32[64,128]{1,0:T(8,128)S(1)} %bitcast.6, f32[4,3,3,16,128]{4,3,2,1,0:T(8,128)S(1)} %get-tuple-element.13.basis, f32[22,8,128]{2,1,0:T(8,128)S(1)} %get-tuple-element.8.own, f32[8,128]{1,0:T(8,128)S(1)} %get-tuple-element.11.table), custom_call_target="tpu_custom_call" | custom-call | flops 100000 | bytes 100000 | tf_op jit(solution)/shard_map/pallas_call | solution.py:405
  (4 shorter events, 0.1 us)
Async XLA Ops:
  0.6 0.7 copy-start.5
  1.3 0.8 %copy-start = (f32[6,2,8,128]{3,2,1,0:T(8,128)S(1)}, f32[6,2,8,128]{3,2,1,0:T(8,128)}, u32[]{:S(2)}) copy-start(f32[6,2,8,128]{3,2,1,0:T(8,128)} %viscous.1) | copy-start | bytes 147460
  2.1 0.7 copy-start.1
  2.8 0.7 copy-start.2
  3.5 0.7 copy-start.3
  4.2 0.7 copy-start.4
  5.0 7.7 %collective-permute-start = (f32[11,8,128]{2,1,0:T(8,128)S(1)}, f32[11,8,128]{2,1,0:T(8,128)S(1)}, u32[]{:S(2)}, u32[]{:S(2)}) collective-permute-start(f32[11,8,128]{2,1,0:T(8,128)S(1)} %get-tuple-element.9), channel_id=1, source_target_pairs={{1,0},{2,1},{3,2},{4,3},{5,4},{6,5},{7,6},{9,8},{10,9},{11,10},{12... | collective-permute-start | bytes 135176 | tf_op jit(solution)/shard_map/ppermute | solution.py:361
  6.3 7.5 %collective-permute-start.1 = (f32[11,8,128]{2,1,0:T(8,128)S(1)}, f32[11,8,128]{2,1,0:T(8,128)S(1)}, u32[]{:S(2)}, u32[]{:S(2)}) collective-permute-start(f32[11,8,128]{2,1,0:T(8,128)S(1)} %get-tuple-element.10), channel_id=1, source_target_pairs={{0,1},{1,2},{2,3},{3,4},{4,5},{5,6},{6,7},{8,9},{9,10},{10,11},{11... | collective-permute-start | bytes 135176 | tf_op jit(solution)/shard_map/ppermute | solution.py:361
  13.8 6.2 %collective-permute-start.3 = (f32[22,16,128]{2,1,0:T(8,128)S(1)}, f32[22,16,128]{2,1,0:T(8,128)S(1)}, u32[]{:S(2)}, u32[]{:S(2)}) collective-permute-start(f32[22,16,128]{2,1,0:T(8,128)S(1)} %shard_map.78.wide), channel_id=1, source_target_pairs={{16,0},{32,16},{48,32},{64,48},{80,64},{96,80},{112,96},{128,112},... | collective-permute-start | bytes 540680 | tf_op jit(solution)/shard_map/ppermute | solution.py:361
  15.1 6.4 %collective-permute-start.2 = (f32[22,16,128]{2,1,0:T(8,128)S(1)}, f32[22,16,128]{2,1,0:T(8,128)S(1)}, u32[]{:S(2)}, u32[]{:S(2)}) collective-permute-start(f32[22,16,128]{2,1,0:T(8,128)S(1)} %shard_map.78.wide), channel_id=1, source_target_pairs={{0,16},{16,32},{32,48},{48,64},{64,80},{80,96},{96,112},{112,128},... | collective-permute-start | bytes 540680 | tf_op jit(solution)/shard_map/ppermute | solution.py:361
  21.5 17.2 %collective-permute-start.4 = (f32[2,22,16,128]{3,2,1,0:T(8,128)S(1)}, f32[2,22,16,128]{3,2,1,0:T(8,128)S(1)}, u32[]{:S(2)}, u32[]{:S(2)}) collective-permute-start(f32[2,22,16,128]{3,2,1,0:T(8,128)S(1)} %shard_map.79), channel_id=1, source_target_pairs={{0,8},{8,0},{1,9},{9,1},{2,10},{10,2},{3,11},{11,3},{4,12},{12,4},... | collective-permute-start | bytes 1081352 | tf_op jit(solution)/shard_map/ppermute | solution.py:388

commit v2 on v1

--- a/solution.py
+++ b/solution.py
@@ -11,19 +11,23 @@
 ROWS = 16
 LAYERS = 10
 FIELDS = 11
+BLOCK = 13
 CLASSES = 16
-TINY_PIVOT = 1e-6
+MOMENTS = 2 * ITERS
+SCALE = 1.0 / 32.0
+TINY_PIVOT = 1e-9
 
 F32 = jnp.float32
 SDS = jax.ShapeDtypeStruct
 VMEM = pl.BlockSpec(memory_space=pltpu.VMEM)
 SMEM = pl.BlockSpec(memory_space=pltpu.SMEM)
+HBM = pl.BlockSpec(memory_space=pltpu.HBM)
 PAIRS = ("ss", "sd", "ds", "dd")
 
 
-def call(body, out_shape, n_in, scratch=(), first_scalar=False, flops=100000):
-    specs = [VMEM] * n_in
-    if first_scalar:
+def call(body, out_shape, n_in, scratch=(), first=None, flops=100000):
+    specs = [VMEM] * n_in if first is not HBM else [HBM] * n_in
+    if first is SMEM:
         specs[0] = SMEM
     many = isinstance(out_shape, (list, tuple))
     return pl.pallas_call(
@@ -37,45 +41,80 @@
     )
 
 
-def pack_body(load, viscous, material, free, moduli, relax, own, low, high, table):
+def pack_body(load, viscous, material, free, moduli, relax, own, low, high, table, kinds, frees, entries, times, done):
+    pairs = (
+        (load, own.at[0:6]),
+        (viscous, own.at[6:18]),
+        (material, kinds),
+        (free, frees),
+        (moduli, entries),
+        (relax, times),
+    )
+    copies = [pltpu.make_async_copy(source, target, done.at[k]) for k, (source, target) in enumerate(pairs)]
+    for copy in copies:
+        copy.start()
+    for copy in copies:
+        copy.wait()
+    row = lax.broadcasted_iota(jnp.int32, (8, 128), 0)
     for field in range(FIELDS):
-        layers = []
-        for layer in range(2):
-            if field < 3:
-                tile = load[field, layer]
-            elif field < 9:
-                tile = viscous[field - 3, layer]
-            elif field == 9:
-                tile = material[layer].astype(F32) - float(CLASSES)
-            else:
-                tile = free[layer].astype(F32)
-            own[2 * field + layer] = tile
-            layers.append(tile)
-        row = lax.broadcasted_iota(jnp.int32, (8, 128), 0)
+        if field == 9:
+            layers = [kinds[layer].astype(F32) - float(CLASSES) for layer in range(2)]
+        elif field == 10:
+            layers = [frees[layer].astype(F32) for layer in range(2)]
+        else:
+            layers = [own[2 * field + layer] for layer in range(2)]
+        if field >= 9:
+            for layer in range(2):
+                own[2 * field + layer] = layers[layer]
         low[field] = jnp.where(row < 4, layers[0], pltpu.roll(layers[1], 4, 0))
         high[field] = jnp.where(row < 4, pltpu.roll(layers[0], 4, 0), layers[1])
-    time = relax[...]
+    time = times[...]
     retain = time / (time + 1.0)
-    arm = moduli[2:3] * retain
-    bound = jnp.max(moduli[0:1] + 2.0 * (moduli[1:2] + arm), axis=1, keepdims=True)
     table[...] = jnp.zeros((8, 128), F32)
-    table[0:1, 0:CLASSES] = moduli[0:1] * (1.0 / 16.0)
-    table[1:2, 0:CLASSES] = moduli[1:2] * (1.0 / 16.0)
-    table[2:3, 0:CLASSES] = arm * (1.0 / 16.0)
+    table[0:1, 0:CLASSES] = entries[0:1] * (1.0 / 16.0)
+    table[1:2, 0:CLASSES] = entries[1:2] * (1.0 / 16.0)
+    table[2:3, 0:CLASSES] = (entries[2:3] * retain) * (1.0 / 16.0)
     table[3:4, 0:CLASSES] = retain
-    table[4:5] = jnp.broadcast_to(1.0 / bound, (1, 128))
-
-
-def widen_body(own, above, below, wide):
+
+
+def pick(table, row, index):
+    entries = jnp.broadcast_to(table[row : row + 1], index.shape)
+    return jnp.take_along_axis(entries, index, axis=1, mode="promise_in_bounds")
+
+
+def widen_body(own, above, below, table, wide):
     row = lax.broadcasted_iota(jnp.int32, (8, 128), 0)
-    for field in range(FIELDS):
+
+    def rows(field):
         upper, lower = above[field], below[field]
-        uppers = (upper, pltpu.roll(upper, 4, 0))
-        lowers = (pltpu.roll(lower, 4, 0), lower)
-        for layer in range(2):
-            k = 2 * field + layer
-            wide[k, 0:8] = own[k]
-            wide[k, 8:16] = jnp.where(row < 4, uppers[layer], lowers[layer])
+        halos = (
+            jnp.where(row < 4, upper, pltpu.roll(lower, 4, 0)),
+            jnp.where(row < 4, pltpu.roll(upper, 4, 0), lower),
+        )
+        return [jnp.concatenate([own[2 * field + layer], halos[layer]], axis=0) for layer in range(2)]
+
+    fields = [rows(field) for field in range(FIELDS)]
+    for layer in range(2):
+        wide[9 + layer] = fields[9][layer]
+        wide[11 + layer] = fields[10][layer]
+    pending = None
+    for layer in range(2):
+        index = fields[9][layer].astype(jnp.int32) + CLASSES
+        factor = 8.0 * pick(table, 2, index)
+        xx, yy, zz, yz, xz, xy = (factor * fields[3 + part][layer] for part in range(6))
+        forces = (
+            {"dss": xx, "ssd": xz, "sds": xy},
+            {"sds": yy, "ssd": yz, "dss": xy},
+            {"ssd": zz, "sds": yz, "dss": xz},
+        )
+        upper, lower = to_nodes(forces)
+        pairs = lower if pending is None else merged(pending, lower)
+        for comp in range(3):
+            force = node_force(pairs[comp])
+            wide[3 * comp + layer] = force if layer == 0 else fields[comp][0] + force
+        pending = upper
+    for comp in range(3):
+        wide[3 * comp + 2] = fields[comp][1] + node_force(pending[comp])
 
 
 def choose_body(core, wide, left, right, out):
@@ -185,42 +224,24 @@
     return [{pair: plus(a[pair], b[pair]) for pair in PAIRS} for a, b in zip(first, second)]
 
 
-def pick(table, row, index):
-    entries = jnp.broadcast_to(table[row : row + 1], (ROWS, 128))
-    return jnp.take_along_axis(entries, index, axis=1, mode="promise_in_bounds")
-
-
-def krylov_body(left, rec, wide, right, table, basis, sums, vec, mask, moduli, images):
+def krylov_body(left, rec, wide, right, table, basis, sums, vec, mask, moduli):
     blocks = (left, rec.at[0], wide, rec.at[1], right)
-
-    def field(number, layer):
-        return blocks[layer // 2][2 * number + layer % 2]
-
-    pending = None
     for layer in range(LAYERS):
-        index = field(9, layer).astype(jnp.int32) + CLASSES
+        block, place = blocks[layer // 2], layer % 2
+        index = block[9 + place].astype(jnp.int32) + CLASSES
         lame, shear, arm = (pick(table, row, index) for row in range(3))
         moduli[0, layer] = lame
         moduli[1, layer] = shear + arm
         moduli[2, layer] = lame * (1.0 / 3.0)
         moduli[3, layer] = shear * (1.0 / 3.0)
         moduli[4, layer] = (lame + 4.0 * shear) * (1.0 / 9.0)
-        mask[layer] = field(10, layer)
-        factor = 8.0 * arm
-        xx, yy, zz, yz, xz, xy = (factor * field(3 + part, layer) for part in range(6))
-        forces = (
-            {"dss": xx, "ssd": xz, "sds": xy},
-            {"sds": yy, "ssd": yz, "dss": xy},
-            {"ssd": zz, "sds": yz, "dss": xz},
-        )
-        upper, lower = to_nodes(forces)
-        if pending is not None:
-            node = layer - 1
-            for comp, pairs in enumerate(merged(pending, lower)):
-                vec[0, comp, node] = mask[node] * (field(comp, node) + node_force(pairs))
-        pending = upper
-
-    scale = jnp.broadcast_to(table[4:5], (ROWS, 128))
+        mask[layer] = block[11 + place]
+        if layer < LAYERS - 1:
+            for comp in range(3):
+                force = block[3 * comp + 1 + place]
+                if place == 1:
+                    force = force + blocks[layer // 2 + 1][3 * comp]
+                vec[0, comp, layer] = mask[layer] * force
 
     def masked_pairs(step, layer):
         return [node_pairs(mask[layer] * vec[step, comp, layer]) for comp in range(3)]
@@ -238,13 +259,7 @@
                 for comp, pairs in enumerate(merged(pending, lower)):
                     value = vec[step, comp, node]
                     image = free * node_force(pairs) + (1.0 - free) * value
-                    if node in (4, 5):
-                        images[step, comp, node - 4] = image[0:8]
-                    if step == 0:
-                        fresh = scale * image - value
-                    else:
-                        fresh = 2.0 * (scale * image - value) - vec[step - 1, comp, node]
-                    vec[step + 1, comp, node] = fresh
+                    vec[step + 1, comp, node] = SCALE * image
             pending = upper
             below = above
 
@@ -265,35 +280,21 @@
             energy = energy + (1.0 - mask[layer, 0:8]) * value * value
         below = above
 
-    def product(first, second):
+    moments = []
+    for k in range(MOMENTS - 1):
         total = None
         for comp in range(3):
-            for layer in range(2):
-                total = plus(total, first(comp, layer) * second(comp, layer))
-        return total
-
-    def vector(step):
-        return lambda comp, layer: vec[step, comp, 4 + layer, 0:8]
-
-    def image(step):
-        return lambda comp, layer: images[step, comp, layer]
-
-    products = []
-    for i in range(ITERS):
-        for j in range(i + 1):
-            if i == last and j == last:
-                products.append(energy)
-            elif i == last:
-                products.append(product(vector(i), image(j)))
-            else:
-                products.append(product(vector(j), image(i)))
-    for i in range(ITERS):
-        products.append(product(vector(0), vector(i)))
-    rows = jnp.zeros((ROWS, 128), F32)
-    for number, value in enumerate(products):
-        rows = jnp.where(iota(0) == number, jnp.sum(value, axis=0, keepdims=True), rows)
-    column = jnp.sum(rows, axis=1, keepdims=True)
-    line = jnp.sum(jnp.where(iota(0) == iota(1), column, 0.0), axis=0, keepdims=True)
+            for layer in (4, 5):
+                total = plus(total, vec[k // 2, comp, layer, 0:8] * vec[(k + 1) // 2, comp, layer, 0:8])
+        moments.append(total)
+    moments.append(SCALE * energy)
+    row, lane = iota(0, (8, 128)), iota(1, (8, 128))
+    rows = jnp.zeros((8, 128), F32)
+    for k, total in enumerate(moments):
+        rows = jnp.where(row == k, jnp.sum(total, axis=0, keepdims=True), rows)
+    for step in (64, 32, 16):
+        rows = rows + pltpu.roll(rows, step, 1)
+    line = jnp.sum(jnp.where(lane // 16 == row, rows, 0.0), axis=0, keepdims=True)
     sums[...] = jnp.broadcast_to(line, sums.shape)
     for step in range(ITERS):
         for comp in range(3):
@@ -301,31 +302,106 @@
                 basis[step, comp, layer] = vec[step, comp, 3 + layer]
 
 
+def two_sum(a, b):
+    total = a + b
+    part = total - a
+    return total, (a - (total - part)) + (b - part)
+
+
+def settle(high, low):
+    total = high + low
+    return total, low - (total - high)
+
+
+def add(a, b):
+    total, rest = two_sum(a[0], b[0])
+    return settle(total, rest + (a[1] + b[1]))
+
+
+def halves(a):
+    wide = 4097.0 * a
+    high = wide - (wide - a)
+    return high, a - high
+
+
+def two_product(a, b):
+    total = a * b
+    (ah, al), (bh, bl) = halves(a), halves(b)
+    return total, ((ah * bh - total) + ah * bl + al * bh) + al * bl
+
+
+def multiply(a, b):
+    total, rest = two_product(a[0], b[0])
+    return settle(total, rest + (a[0] * b[1] + a[1] * b[0]))
+
+
+def subtract(a, b):
+    return add(a, (-b[0], -b[1]))
+
+
+def invert(a):
+    first = 1.0 / a[0]
+    total, rest = two_product(a[0], first)
+    return settle(first, first * (((1.0 - total) - rest) - a[1] * first))
+
+
+def rolled(a, steps, axis):
+    return tuple(pltpu.roll(part, steps, axis) for part in a)
+
+
+def over_rows(pair):
+    for step in (4, 2, 1):
+        pair = add(pair, rolled(pair, step, 0))
+    return pair
+
+
+def total_of(pairs):
+    while len(pairs) > 1:
+        pairs = [add(*pairs[k : k + 2]) if k + 1 < len(pairs) else pairs[k] for k in range(0, len(pairs), 2)]
+    return pairs[0]
+
+
+def middle_body(sums, out):
+    pair = over_rows(total_of([(sums[k : k + 8], jnp.zeros((8, 128), F32)) for k in range(0, sums.shape[0], 8)]))
+    high, low = add(pair, rolled(pair, 120, 1))
+    line = jnp.where(iota(1, (8, 128)) % 16 < 8, high, pltpu.roll(low, 8, 1))
+    for k in range(0, out.shape[0], 8):
+        count = min(8, out.shape[0] - k)
+        out[k : k + count] = line[0:count]
+
+
 def final_body(sums, basis, own, table, displacement, viscous_next):
-    line = jnp.sum(sums[...], axis=0, keepdims=True)
-    lane = iota(1, (1, 128))
-
-    def entry(number):
-        return jnp.sum(jnp.where(lane == number, line, 0.0), axis=1, keepdims=True)
-
-    matrix = [[entry(i * (i + 1) // 2 + j) for j in range(i + 1)] for i in range(ITERS)]
-    value = [entry(10 + i) for i in range(ITERS)]
-    first = [matrix[i][i] for i in range(ITERS)]
+    pairs = []
+    for k in range(sums.shape[0] // 8):
+        tile = sums[8 * k : 8 * k + 8]
+        pairs.append((tile, pltpu.roll(tile, 120, 1)))
+    pair = over_rows(total_of(pairs))
+    for step in (4, 2, 1):
+        pair = add(pair, rolled(pair, 128 - step, 1))
+
+    def moment(k):
+        index = jnp.full((8, 128), 16 * k, jnp.int32)
+        return tuple(jnp.take_along_axis(part, index, axis=1, mode="promise_in_bounds") for part in pair)
+
+    moments = [moment(k) for k in range(MOMENTS)]
+    matrix = [[moments[i + j + 1] for j in range(i + 1)] for i in range(ITERS)]
+    value = moments[:ITERS]
     ratio = {}
     inverse = []
     for k in range(ITERS):
         pivot = matrix[k][k]
-        inverse.append(jnp.where(pivot > TINY_PIVOT * first[k], 1.0 / pivot, 0.0))
+        kept = pivot[0] > TINY_PIVOT * moments[2 * k + 1][0]
+        inverse.append(tuple(jnp.where(kept, part, 0.0) for part in invert(pivot)))
         for i in range(k + 1, ITERS):
-            ratio[i, k] = matrix[i][k] * inverse[k]
+            ratio[i, k] = multiply(matrix[i][k], inverse[k])
             for j in range(k + 1, i + 1):
-                matrix[i][j] = matrix[i][j] - ratio[i, k] * matrix[j][k]
-            value[i] = value[i] - ratio[i, k] * value[k]
-    value = [value[k] * inverse[k] for k in range(ITERS)]
+                matrix[i][j] = subtract(matrix[i][j], multiply(ratio[i, k], matrix[j][k]))
+            value[i] = subtract(value[i], multiply(ratio[i, k], value[k]))
+    value = [multiply(value[k], inverse[k]) for k in range(ITERS)]
     for k in reversed(range(ITERS)):
         for i in range(k):
-            value[i] = value[i] - ratio[k, i] * value[k]
-    weights = [jnp.broadcast_to(v, (ROWS, 128)) for v in value]
+            value[i] = subtract(value[i], multiply(ratio[k, i], value[k]))
+    weights = [SCALE * jnp.concatenate([v[0], v[0]], axis=0) for v in value]
 
     pairs = []
     for layer in range(3):
@@ -361,10 +437,6 @@
     return lax.ppermute(value, axes, pairs)
 
 
-def summed(value, axes):
-    return jnp.sum(lax.all_to_all(value, axes, 0, 0), axis=0)
-
-
 def solution(mesh):
     count_x, count_z = mesh.shape["gx"], mesh.shape["gy"]
     along = min(8, count_x // 2)
@@ -377,14 +449,34 @@
             pack_body,
             (SDS((22, 8, 128), F32), SDS((11, 8, 128), F32), SDS((11, 8, 128), F32), SDS((8, 128), F32)),
             6,
-        )(load, viscous, material, free_nodes, moduli_table, relax_time.reshape(1, -1))
+            scratch=(
+                pltpu.VMEM((2, 8, 128), jnp.int32),
+                pltpu.VMEM((2, 8, 128), jnp.int32),
+                pltpu.VMEM((3, CLASSES), F32),
+                pltpu.VMEM((1, CLASSES), F32),
+                pltpu.SemaphoreType.DMA((6,)),
+            ),
+            first=HBM,
+        )(
+            *(
+                pltpu.with_memory_space_constraint(value, pltpu.HBM)
+                for value in (
+                    load.reshape(6, 8, 128),
+                    viscous.reshape(12, 8, 128),
+                    material,
+                    free_nodes,
+                    moduli_table,
+                    relax_time.reshape(1, CLASSES),
+                )
+            )
+        )
         below = shifted(high, ("z",), count_z, 1)
         above = shifted(low, ("z",), count_z, -1)
-        wide = call(widen_body, SDS((22, ROWS, 128), F32), 3)(own, above, below)
+        wide = call(widen_body, SDS((BLOCK, ROWS, 128), F32), 4)(own, above, below, table)
         left = shifted(wide, ("y", "x"), chips, 1)
         right = shifted(wide, ("y", "x"), chips, -1)
         core = lax.axis_index("core").astype(jnp.int32).reshape(1)
-        given = call(choose_body, SDS((2, 22, ROWS, 128), F32), 4, first_scalar=True)(core, wide, left, right)
+        given = call(choose_body, SDS((2, BLOCK, ROWS, 128), F32), 4, first=SMEM)(core, wide, left, right)
         taken = lax.ppermute(given, ("core",), [(0, 1), (1, 0)])
         near, far = 2 * along, across * count_z
         basis, sums = call(
@@ -395,15 +487,15 @@
                 pltpu.VMEM((ITERS, 3, LAYERS, ROWS, 128), F32),
                 pltpu.VMEM((LAYERS, ROWS, 128), F32),
                 pltpu.VMEM((5, LAYERS, ROWS, 128), F32),
-                pltpu.VMEM((ITERS - 1, 3, 2, 8, 128), F32),
             ),
             flops=20000000,
         )(left, taken, wide, right, table)
-        partial = summed(sums.reshape(near, 1, 128), ("x", "core"))
-        everything = lax.all_to_all(jnp.broadcast_to(partial[None], (far, 1, 128)), ("y", "z"), 0, 0)
+        group = lax.all_to_all(sums.reshape(near, 1, 128), ("x", "core"), 0, 0)
+        partial = call(middle_body, SDS((far, 128), F32), 1)(group.reshape(near, 128))
+        everything = lax.all_to_all(partial.reshape(far, 1, 128), ("y", "z"), 0, 0)
         return tuple(
             call(final_body, (SDS((3, 2, 8, 128), F32), SDS((6, 2, 8, 128), F32)), 4)(
-                everything.reshape(far, 128), basis, own, table
+                jnp.pad(everything.reshape(far, 128), ((0, -far % 8), (0, 0))), basis, own, table
             )
         )
 

time: 79.6 us -> 75.2 us (0.945)
  local copies, waits for them, and re-layouts: 4.28 us -> 0 us
  Pallas kernels: 3.04 us -> 4.11 us
  waiting for transfers between devices: 4.8 us -> 3.87 us
    unnamed x12 -> x0, local copies, waits for them, and re-layouts: 4.26 us -> none
    pallas_call x1, Pallas kernels: 0.1 us -> 0.89 us  [shards(): call(pack_body, (SDS((22, 8, 128), F32), SDS((11, 8, 128), F32), SDS((11,...]
where the time goes in v2:
time: 75.2 us; the launch traced here: 74.8 us
  blocking collectives  37.2 us (49%)
  starting transfers between devices  28.9 us (38%)
  Pallas kernels  4.11 us (5%)
  waiting for transfers between devices  3.87 us (5%)
    all_to_all x1, blocking collectives, shards(): everything = lax.all_to_all(partial.reshape(far, 1, 128), ('y', 'z'), 0, 0)  26.3 us
    ppermute x1, starting transfers between devices, shards(): taken = lax.ppermute(given, ('core',), [(0, 1), (1, 0)])  16 us
    ppermute x4, starting transfers between devices, shifted(): return lax.ppermute(value, axes, pairs)  12.9 us
    all_to_all x1, blocking collectives, shards(): group = lax.all_to_all(sums.reshape(near, 1, 128), ('x', 'core'), 0, 0)  10.9 us
    ppermute x4, waiting for transfers between devices, shifted(): return lax.ppermute(value, axes, pairs)  2.8 us
  transfers between devices with their start and end apart: 5, of which 4 were waited for; matrix products, arithmetic and copies ran while one was open for 0% of the time, Pallas kernels for 0%

profile of v2, /device:TPU:1, one launch (start us, length us, event | category | flops | bytes accessed | tf_op | source)
XLA Modules:
  0.0 74.8 jit_solution(4759062331644163588)
XLA Ops:
  0.6 0.9 %shard_map.77 = (f32[22,8,128]{2,1,0:T(8,128)S(1)}, f32[11,8,128]{2,1,0:T(8,128)S(1)}, f32[11,8,128]{2,1,0:T(8,128)S(1)}, f32[8,128]{1,0:T(8,128)S(1)}) custom-call(f32[6,8,128]{2,1,0:T(8,128)} %bitcast.17, f32[12,8,128]{2,1,0:T(8,128)} %bitcast.16, s32[2,8,128]{2,1,0:T(8,128)} %material.1, s32[2,8,128]{2,1,0:T(8,128)} %free.1, f32[3,16]{1,0:T(4,128)} %moduli.1, ...), custom_call_target="tpu_custom_call" | custom-call | flops 100000 | bytes 100000 | tf_op jit(solution)/shard_map/pallas_call | solution.py:448
  1.5 1.3 %collective-permute-start = (f32[11,8,128]{2,1,0:T(8,128)S(1)}, f32[11,8,128]{2,1,0:T(8,128)S(1)}, u32[]{:S(2)}, u32[]{:S(2)}) collective-permute-start(f32[11,8,128]{2,1,0:T(8,128)S(1)} %get-tuple-element.9), channel_id=1, source_target_pairs={{1,0},{2,1},{3,2},{4,3},{5,4},{6,5},{7,6},{9,8},{10,9},{11,10},{12... | collective-permute-start | bytes 135176 | tf_op jit(solution)/shard_map/ppermute | solution.py:437
  2.8 6.4 %collective-permute-start.1 = (f32[11,8,128]{2,1,0:T(8,128)S(1)}, f32[11,8,128]{2,1,0:T(8,128)S(1)}, u32[]{:S(2)}, u32[]{:S(2)}) collective-permute-start(f32[11,8,128]{2,1,0:T(8,128)S(1)} %get-tuple-element.10), channel_id=1, source_target_pairs={{0,1},{1,2},{2,3},{3,4},{4,5},{5,6},{6,7},{8,9},{9,10},{10,11},{11... | collective-permute-start | bytes 135176 | tf_op jit(solution)/shard_map/ppermute | solution.py:437
  9.2 0.0 collective-permute-done.above
  9.2 1.1 %collective-permute-done.1.below = f32[11,8,128]{2,1,0:T(8,128)S(1)} collective-permute-done((f32[11,8,128]{2,1,0:T(8,128)S(1)}, f32[11,8,128]{2,1,0:T(8,128)S(1)}, u32[]{:S(2)}, u32[]{:S(2)}) %collective-permute-start.1) | collective-permute-done | bytes 45088 | tf_op jit(solution)/shard_map/ppermute | solution.py:437
  10.3 0.2 shard_map.78.wide
  10.5 1.3 %collective-permute-start.3 = (f32[13,16,128]{2,1,0:T(8,128)S(1)}, f32[13,16,128]{2,1,0:T(8,128)S(1)}, u32[]{:S(2)}, u32[]{:S(2)}) collective-permute-start(f32[13,16,128]{2,1,0:T(8,128)S(1)} %shard_map.78.wide), channel_id=1, source_target_pairs={{16,0},{32,16},{48,32},{64,48},{80,64},{96,80},{112,96},{128,112},... | collective-permute-start | bytes 319496 | tf_op jit(solution)/shard_map/ppermute | solution.py:437
  11.8 4.0 %collective-permute-start.2 = (f32[13,16,128]{2,1,0:T(8,128)S(1)}, f32[13,16,128]{2,1,0:T(8,128)S(1)}, u32[]{:S(2)}, u32[]{:S(2)}) collective-permute-start(f32[13,16,128]{2,1,0:T(8,128)S(1)} %shard_map.78.wide), channel_id=1, source_target_pairs={{0,16},{16,32},{32,48},{48,64},{64,80},{80,96},{96,112},{112,128},... | collective-permute-start | bytes 319496 | tf_op jit(solution)/shard_map/ppermute | solution.py:437
  15.8 0.1 collective-permute-done.3.right
  16.0 1.5 %collective-permute-done.2.left = f32[13,16,128]{2,1,0:T(8,128)S(1)} collective-permute-done((f32[13,16,128]{2,1,0:T(8,128)S(1)}, f32[13,16,128]{2,1,0:T(8,128)S(1)}, u32[]{:S(2)}, u32[]{:S(2)}) %collective-permute-start.2) | collective-permute-done | bytes 106528 | tf_op jit(solution)/shard_map/ppermute | solution.py:437
  17.5 16.0 %collective-permute-start.4 = (f32[2,13,16,128]{3,2,1,0:T(8,128)S(1)}, f32[2,13,16,128]{3,2,1,0:T(8,128)S(1)}, u32[]{:S(2)}, u32[]{:S(2)}) collective-permute-start(f32[2,13,16,128]{3,2,1,0:T(8,128)S(1)} %shard_map.79), channel_id=1, source_target_pairs={{0,8},{8,0},{1,9},{9,1},{2,10},{10,2},{3,11},{11,3},{4,12},{12,4},... | collective-permute-start | bytes 638984 | tf_op jit(solution)/shard_map/ppermute | solution.py:480
  33.5 1.1 %collective-permute-done.4.rec = f32[2,13,16,128]{3,2,1,0:T(8,128)S(1)} collective-permute-done((f32[2,13,16,128]{3,2,1,0:T(8,128)S(1)}, f32[2,13,16,128]{3,2,1,0:T(8,128)S(1)}, u32[]{:S(2)}, u32[]{:S(2)}) %collective-permute-start.4) | collective-permute-done | bytes 213024 | tf_op jit(solution)/shard_map/ppermute | solution.py:480
  34.6 1.5 %shard_map.80 = (f32[4,3,3,16,128]{4,3,2,1,0:T(8,128)S(1)}, f32[16,128]{1,0:T(8,128)S(1)}) custom-call(f32[13,16,128]{2,1,0:T(8,128)S(1)} %collective-permute-done.2.left, f32[2,13,16,128]{3,2,1,0:T(8,128)S(1)} %collective-permute-done.4.rec, f32[13,16,128]{2,1,0:T(8,128)S(1)} %shard_map.78.wide, f32[13,16,128]{2,1,0:T(8,128)S(1)} %collective-permute-done.3.right, ...), custom_call_target="tpu_custom_call" | custom-call | flops 20000000 | bytes 100000 | tf_op jit(solution)/shard_map/pallas_call | solution.py:482
  36.0 10.9 %all_to_all.10 = f32[16,1,128]{2,1,0:T(1,128)S(1)} all-to-all(f32[16,1,128]{2,1,0:T(1,128)S(1)} %bitcast.15), channel_id=1, replica_groups=mesh['y'=8,'x'=8,'core'=2,'z'=8] {'x','core'}, dimensions={0} | all-to-all | bytes 16384 | tf_op jit(solution)/shard_map/all_to_all | solution.py:493
  46.9 0.2 shard_map.81
  47.1 26.3 %all_to_all.11 = f32[64,1,128]{2,1,0:T(1,128)S(1)} all-to-all(f32[64,1,128]{2,1,0:T(1,128)S(1)} %bitcast.13), channel_id=1, replica_groups=mesh['y'=8,'x'=8,'core'=2,'z'=8] {'y','z'}, dimensions={0} | all-to-all | bytes 65536 | tf_op jit(solution)/shard_map/all_to_all | solution.py:495
  73.5 1.4 %shard_map.82 = (f32[3,2,8,128]{3,2,1,0:T(8,128)}, f32[6,2,8,128]{3,2,1,0:T(8,128)}) custom-call(f32[64,128]{1,0:T(8,128)S(1)} %bitcast.12, f32[4,3,3,16,128]{4,3,2,1,0:T(8,128)S(1)} %get-tuple-element.13.basis, f32[22,8,128]{2,1,0:T(8,128)S(1)} %get-tuple-element.8.own, f32[8,128]{1,0:T(8,128)S(1)} %get-tuple-element.11.table), custom_call_target="tpu_custom_call" | custom-call | flops 100000 | bytes 100000 | tf_op jit(solution)/shard_map/pallas_call | solution.py:497
  (1 shorter events, 0.0 us)
Async XLA Ops:
  1.5 7.7 %collective-permute-start = (f32[11,8,128]{2,1,0:T(8,128)S(1)}, f32[11,8,128]{2,1,0:T(8,128)S(1)}, u32[]{:S(2)}, u32[]{:S(2)}) collective-permute-start(f32[11,8,128]{2,1,0:T(8,128)S(1)} %get-tuple-element.9), channel_id=1, source_target_pairs={{1,0},{2,1},{3,2},{4,3},{5,4},{6,5},{7,6},{9,8},{10,9},{11,10},{12... | collective-permute-start | bytes 135176 | tf_op jit(solution)/shard_map/ppermute | solution.py:437
  2.8 7.5 %collective-permute-start.1 = (f32[11,8,128]{2,1,0:T(8,128)S(1)}, f32[11,8,128]{2,1,0:T(8,128)S(1)}, u32[]{:S(2)}, u32[]{:S(2)}) collective-permute-start(f32[11,8,128]{2,1,0:T(8,128)S(1)} %get-tuple-element.10), channel_id=1, source_target_pairs={{0,1},{1,2},{2,3},{3,4},{4,5},{5,6},{6,7},{8,9},{9,10},{10,11},{11... | collective-permute-start | bytes 135176 | tf_op jit(solution)/shard_map/ppermute | solution.py:437
  10.5 5.4 %collective-permute-start.3 = (f32[13,16,128]{2,1,0:T(8,128)S(1)}, f32[13,16,128]{2,1,0:T(8,128)S(1)}, u32[]{:S(2)}, u32[]{:S(2)}) collective-permute-start(f32[13,16,128]{2,1,0:T(8,128)S(1)} %shard_map.78.wide), channel_id=1, source_target_pairs={{16,0},{32,16},{48,32},{64,48},{80,64},{96,80},{112,96},{128,112},... | collective-permute-start | bytes 319496 | tf_op jit(solution)/shard_map/ppermute | solution.py:437
  11.8 5.7 %collective-permute-start.2 = (f32[13,16,128]{2,1,0:T(8,128)S(1)}, f32[13,16,128]{2,1,0:T(8,128)S(1)}, u32[]{:S(2)}, u32[]{:S(2)}) collective-permute-start(f32[13,16,128]{2,1,0:T(8,128)S(1)} %shard_map.78.wide), channel_id=1, source_target_pairs={{0,16},{16,32},{32,48},{48,64},{64,80},{80,96},{96,112},{112,128},... | collective-permute-start | bytes 319496 | tf_op jit(solution)/shard_map/ppermute | solution.py:437
  17.5 17.0 %collective-permute-start.4 = (f32[2,13,16,128]{3,2,1,0:T(8,128)S(1)}, f32[2,13,16,128]{3,2,1,0:T(8,128)S(1)}, u32[]{:S(2)}, u32[]{:S(2)}) collective-permute-start(f32[2,13,16,128]{3,2,1,0:T(8,128)S(1)} %shard_map.79), channel_id=1, source_target_pairs={{0,8},{8,0},{1,9},{9,1},{2,10},{10,2},{3,11},{11,3},{4,12},{12,4},... | collective-permute-start | bytes 638984 | tf_op jit(solution)/shard_map/ppermute | solution.py:480

commit v3 on v2

--- a/solution.py
+++ b/solution.py
@@ -25,15 +25,12 @@
 PAIRS = ("ss", "sd", "ds", "dd")
 
 
-def call(body, out_shape, n_in, scratch=(), first=None, flops=100000):
-    specs = [VMEM] * n_in if first is not HBM else [HBM] * n_in
-    if first is SMEM:
-        specs[0] = SMEM
+def call(body, out_shape, n_in, scratch=(), spec=VMEM, scalars=0, flops=100000):
     many = isinstance(out_shape, (list, tuple))
     return pl.pallas_call(
         body,
         out_shape=out_shape,
-        in_specs=specs,
+        in_specs=[SMEM] * scalars + [spec] * (n_in - scalars),
         out_specs=[VMEM] * len(out_shape) if many else VMEM,
         scratch_shapes=list(scratch),
         compiler_params=pltpu.CompilerParams(vmem_limit_bytes=24 * 1024 * 1024),
@@ -41,7 +38,9 @@
     )
 
 
-def pack_body(load, viscous, material, free, moduli, relax, own, low, high, table, kinds, frees, entries, times, done):
+def pack_body(
+    odd, load, viscous, material, free, moduli, relax, own, first, second, table, kinds, frees, entries, times, done
+):
     pairs = (
         (load, own.at[0:6]),
         (viscous, own.at[6:18]),
@@ -56,6 +55,7 @@
     for copy in copies:
         copy.wait()
     row = lax.broadcasted_iota(jnp.int32, (8, 128), 0)
+    even = jnp.full((8, 128), odd[0], jnp.int32) == 0
     for field in range(FIELDS):
         if field == 9:
             layers = [kinds[layer].astype(F32) - float(CLASSES) for layer in range(2)]
@@ -66,8 +66,10 @@
         if field >= 9:
             for layer in range(2):
                 own[2 * field + layer] = layers[layer]
-        low[field] = jnp.where(row < 4, layers[0], pltpu.roll(layers[1], 4, 0))
-        high[field] = jnp.where(row < 4, pltpu.roll(layers[0], 4, 0), layers[1])
+        low = jnp.where(row < 4, layers[0], pltpu.roll(layers[1], 4, 0))
+        high = jnp.where(row < 4, pltpu.roll(layers[0], 4, 0), layers[1])
+        first[field] = jnp.where(even, high, low)
+        second[field] = jnp.where(even, low, high)
     time = times[...]
     retain = time / (time + 1.0)
     table[...] = jnp.zeros((8, 128), F32)
@@ -82,11 +84,13 @@
     return jnp.take_along_axis(entries, index, axis=1, mode="promise_in_bounds")
 
 
-def widen_body(own, above, below, table, wide):
+def widen_body(odd, own, first, second, table, wide):
     row = lax.broadcasted_iota(jnp.int32, (8, 128), 0)
+    even = jnp.full((8, 128), odd[0], jnp.int32) == 0
 
     def rows(field):
-        upper, lower = above[field], below[field]
+        upper = jnp.where(even, first[field], second[field])
+        lower = jnp.where(even, second[field], first[field])
         halos = (
             jnp.where(row < 4, upper, pltpu.roll(lower, 4, 0)),
             jnp.where(row < 4, pltpu.roll(upper, 4, 0), lower),
@@ -117,16 +121,26 @@
         wide[3 * comp + 2] = fields[comp][1] + node_force(pending[comp])
 
 
-def choose_body(core, wide, left, right, out):
+def choose_body(core, odd, wide, first, second, given, sides):
+    @pl.when(odd[0] == 0)
+    def _():
+        sides[0] = second[...]
+        sides[1] = first[...]
+
+    @pl.when(odd[0] != 0)
+    def _():
+        sides[0] = first[...]
+        sides[1] = second[...]
+
     @pl.when(core[0] == 0)
     def _():
-        out[0] = wide[...]
-        out[1] = right[...]
+        given[0] = wide[...]
+        given[1] = sides[1]
 
     @pl.when(core[0] != 0)
     def _():
-        out[0] = left[...]
-        out[1] = wide[...]
+        given[0] = sides[0]
+        given[1] = wide[...]
 
 
 def iota(axis, shape=(ROWS, 128)):
@@ -224,8 +238,8 @@
     return [{pair: plus(a[pair], b[pair]) for pair in PAIRS} for a, b in zip(first, second)]
 
 
-def krylov_body(left, rec, wide, right, table, basis, sums, vec, mask, moduli):
-    blocks = (left, rec.at[0], wide, rec.at[1], right)
+def krylov_body(sides, rec, wide, table, basis, sums, vec, mask, moduli):
+    blocks = (sides.at[0], rec.at[0], wide, rec.at[1], sides.at[1])
     for layer in range(LAYERS):
         block, place = blocks[layer // 2], layer % 2
         index = block[9 + place].astype(jnp.int32) + CLASSES
@@ -432,9 +446,9 @@
             viscous_next[part, layer] = retain * old + (1.0 - retain) * strain[part][0:8]
 
 
-def shifted(value, axes, count, steps):
-    pairs = [(i, i + steps) for i in range(count) if 0 <= i + steps < count]
-    return lax.ppermute(value, axes, pairs)
+def swapped(value, axes, count, start):
+    lower = [i for i in range(start, count - 1, 2)]
+    return lax.ppermute(value, axes, [(i, i + 1) for i in lower] + [(i + 1, i) for i in lower])
 
 
 def solution(mesh):
@@ -445,10 +459,14 @@
     chips = along * across
 
     def shards(load, viscous, material, free_nodes, moduli_table, relax_time):
-        own, low, high, table = call(
+        def parity(axes):
+            return (lax.axis_index(axes) % 2).astype(jnp.int32).reshape(1)
+
+        odd_row, odd_chip, core = parity("z"), parity("x"), parity("core")
+        own, first, second, table = call(
             pack_body,
             (SDS((22, 8, 128), F32), SDS((11, 8, 128), F32), SDS((11, 8, 128), F32), SDS((8, 128), F32)),
-            6,
+            7,
             scratch=(
                 pltpu.VMEM((2, 8, 128), jnp.int32),
                 pltpu.VMEM((2, 8, 128), jnp.int32),
@@ -456,8 +474,10 @@
                 pltpu.VMEM((1, CLASSES), F32),
                 pltpu.SemaphoreType.DMA((6,)),
             ),
-            first=HBM,
+            spec=HBM,
+            scalars=1,
         )(
+            odd_row,
             *(
                 pltpu.with_memory_space_constraint(value, pltpu.HBM)
                 for value in (
@@ -470,26 +490,30 @@
                 )
             )
         )
-        below = shifted(high, ("z",), count_z, 1)
-        above = shifted(low, ("z",), count_z, -1)
-        wide = call(widen_body, SDS((BLOCK, ROWS, 128), F32), 4)(own, above, below, table)
-        left = shifted(wide, ("y", "x"), chips, 1)
-        right = shifted(wide, ("y", "x"), chips, -1)
-        core = lax.axis_index("core").astype(jnp.int32).reshape(1)
-        given = call(choose_body, SDS((2, BLOCK, ROWS, 128), F32), 4, first=SMEM)(core, wide, left, right)
+        first = swapped(first, ("z",), count_z, 0)
+        second = swapped(second, ("z",), count_z, 1)
+        wide = call(widen_body, SDS((BLOCK, ROWS, 128), F32), 5, scalars=1)(odd_row, own, first, second, table)
+        first = swapped(wide, ("y", "x"), chips, 0)
+        second = swapped(wide, ("y", "x"), chips, 1)
+        given, sides = call(
+            choose_body,
+            (SDS((2, BLOCK, ROWS, 128), F32), SDS((2, BLOCK, ROWS, 128), F32)),
+            5,
+            scalars=2,
+        )(core, odd_chip, wide, first, second)
         taken = lax.ppermute(given, ("core",), [(0, 1), (1, 0)])
         near, far = 2 * along, across * count_z
         basis, sums = call(
             krylov_body,
             (SDS((ITERS, 3, 3, ROWS, 128), F32), SDS((near, 128), F32)),
-            5,
+            4,
             scratch=(
                 pltpu.VMEM((ITERS, 3, LAYERS, ROWS, 128), F32),
                 pltpu.VMEM((LAYERS, ROWS, 128), F32),
                 pltpu.VMEM((5, LAYERS, ROWS, 128), F32),
             ),
             flops=20000000,
-        )(left, taken, wide, right, table)
+        )(sides, taken, wide, table)
         group = lax.all_to_all(sums.reshape(near, 1, 128), ("x", "core"), 0, 0)
         partial = call(middle_body, SDS((far, 128), F32), 1)(group.reshape(near, 128))
         everything = lax.all_to_all(partial.reshape(far, 1, 128), ("y", "z"), 0, 0)

time: 75.2 us -> 75.8 us (level)
  blocking collectives: 37.2 us -> 40.2 us
  starting transfers between devices: 28.9 us -> 26.4 us
    all_to_all x1, blocking collectives: 26.3 us -> 30.4 us  [shards(): everything = lax.all_to_all(partial.reshape(far, 1, 128), ('y', 'z'), 0, 0)]
    ppermute x1, starting transfers between devices: 16 us -> 13.8 us  [shards(): taken = lax.ppermute(given, ('core',), [(0, 1), (1, 0)])]
    all_to_all x1, blocking collectives: 10.9 us -> 9.81 us  [shards(): group = lax.all_to_all(sums.reshape(near, 1, 128), ('x', 'core'), 0, 0)]
  transfers between devices with their start and end apart: 5 -> 5, of which waited for: 4 -> 3; matrix products, arithmetic and copies ran while one was open for 0% -> 0% of each run, Pallas kernels for 0% -> 0%
where the time goes in v3:
time: 75.8 us; the launch traced here: 75.4 us
  blocking collectives  40.2 us (53%)
  starting transfers between devices  26.4 us (35%)
  Pallas kernels  4.15 us (5%)
  waiting for transfers between devices  3.87 us (5%)
    all_to_all x1, blocking collectives, shards(): everything = lax.all_to_all(partial.reshape(far, 1, 128), ('y', 'z'), 0, 0)  30.4 us
    ppermute x1, starting transfers between devices, shards(): taken = lax.ppermute(given, ('core',), [(0, 1), (1, 0)])  13.8 us
    ppermute x4, starting transfers between devices, swapped(): lax.ppermute(value, axes, [(i, i + 1) for i in lower] + [(i + 1, i) for i...  12.6 us
    all_to_all x1, blocking collectives, shards(): group = lax.all_to_all(sums.reshape(near, 1, 128), ('x', 'core'), 0, 0)  9.81 us
    ppermute x4, waiting for transfers between devices, swapped(): lax.ppermute(value, axes, [(i, i + 1) for i in lower] + [(i + 1, i) for i...  2.8 us
  transfers between devices with their start and end apart: 5, of which 3 were waited for; matrix products, arithmetic and copies ran while one was open for 0% of the time, Pallas kernels for 0%

profile of v3, /device:TPU:1, one launch (start us, length us, event | category | flops | bytes accessed | tf_op | source)
XLA Modules:
  0.0 75.4 jit_solution(258982638742545433)
XLA Ops:
  0.6 0.9 %shard_map.77 = (f32[22,8,128]{2,1,0:T(8,128)S(1)}, f32[11,8,128]{2,1,0:T(8,128)S(1)}, f32[11,8,128]{2,1,0:T(8,128)S(1)}, f32[8,128]{1,0:T(8,128)S(1)}) custom-call(s32[1]{0:T(128)} %bitcast.2.odd, f32[6,8,128]{2,1,0:T(8,128)} %bitcast.19, f32[12,8,128]{2,1,0:T(8,128)} %bitcast.18, s32[2,8,128]{2,1,0:T(8,128)} %material.1, s32[2,8,128]{2,1,0:T(8,128)} %free.1, ...), custom_call_target="tpu_custom_call" | custom-call | flops 100000 | bytes 100000 | tf_op jit(solution)/shard_map/pallas_call | solution.py:466
  1.5 5.7 %collective-permute-start = (f32[11,8,128]{2,1,0:T(8,128)S(1)}, f32[11,8,128]{2,1,0:T(8,128)S(1)}, u32[]{:S(2)}, u32[]{:S(2)}) collective-permute-start(f32[11,8,128]{2,1,0:T(8,128)S(1)} %get-tuple-element.11), channel_id=1, source_target_pairs={{0,1},{2,3},{4,5},{6,7},{1,0},{3,2},{5,4},{7,6},{8,9},{10,11},{12,... | collective-permute-start | bytes 135176 | tf_op jit(solution)/shard_map/ppermute | solution.py:451
  7.3 0.7 collective-permute-start.1
  8.0 0.7 collective-permute-done.first
  8.7 0.0 collective-permute-done.1.second
  8.7 0.2 shard_map.78.wide
  8.9 0.7 collective-permute-start.3
  9.6 5.6 %collective-permute-start.2 = (f32[13,16,128]{2,1,0:T(8,128)S(1)}, f32[13,16,128]{2,1,0:T(8,128)S(1)}, u32[]{:S(2)}, u32[]{:S(2)}) collective-permute-start(f32[13,16,128]{2,1,0:T(8,128)S(1)} %shard_map.78.wide), channel_id=1, source_target_pairs={{0,16},{32,48},{64,80},{96,112},{128,144},{160,176},{192,208},{224... | collective-permute-start | bytes 319496 | tf_op jit(solution)/shard_map/ppermute | solution.py:451
  15.2 0.0 collective-permute-done.3.second
  15.2 2.1 %collective-permute-done.2.first = f32[13,16,128]{2,1,0:T(8,128)S(1)} collective-permute-done((f32[13,16,128]{2,1,0:T(8,128)S(1)}, f32[13,16,128]{2,1,0:T(8,128)S(1)}, u32[]{:S(2)}, u32[]{:S(2)}) %collective-permute-start.2) | collective-permute-done | bytes 106528 | tf_op jit(solution)/shard_map/ppermute | solution.py:451
  17.3 13.8 %collective-permute-start.4 = (f32[2,13,16,128]{3,2,1,0:T(8,128)S(1)}, f32[2,13,16,128]{3,2,1,0:T(8,128)S(1)}, u32[]{:S(2)}, u32[]{:S(2)}) collective-permute-start(f32[2,13,16,128]{3,2,1,0:T(8,128)S(1)} %get-tuple-element.15), channel_id=1, source_target_pairs={{0,8},{8,0},{1,9},{9,1},{2,10},{10,2},{3,11},{11,3},{4,12},{12,4},... | collective-permute-start | bytes 638984 | tf_op jit(solution)/shard_map/ppermute | solution.py:504
  31.1 1.1 %collective-permute-done.4.rec = f32[2,13,16,128]{3,2,1,0:T(8,128)S(1)} collective-permute-done((f32[2,13,16,128]{3,2,1,0:T(8,128)S(1)}, f32[2,13,16,128]{3,2,1,0:T(8,128)S(1)}, u32[]{:S(2)}, u32[]{:S(2)}) %collective-permute-start.4) | collective-permute-done | bytes 213024 | tf_op jit(solution)/shard_map/ppermute | solution.py:504
  32.2 1.5 %shard_map.80 = (f32[4,3,3,16,128]{4,3,2,1,0:T(8,128)S(1)}, f32[16,128]{1,0:T(8,128)S(1)}) custom-call(f32[2,13,16,128]{3,2,1,0:T(8,128)S(1)} %get-tuple-element.14.sides, f32[2,13,16,128]{3,2,1,0:T(8,128)S(1)} %collective-permute-done.4.rec, f32[13,16,128]{2,1,0:T(8,128)S(1)} %shard_map.78.wide, f32[8,128]{1,0:T(8,128)S(1)} %get-tuple-element.13.table), custom_call_target="tpu_custom_call" | custom-call | flops 20000000 | bytes 100000 | tf_op jit(solution)/shard_map/pallas_call | solution.py:506
  33.6 9.8 %all_to_all.10 = f32[16,1,128]{2,1,0:T(1,128)S(1)} all-to-all(f32[16,1,128]{2,1,0:T(1,128)S(1)} %bitcast.17), channel_id=1, replica_groups=mesh['y'=8,'x'=8,'core'=2,'z'=8] {'x','core'}, dimensions={0} | all-to-all | bytes 16384 | tf_op jit(solution)/shard_map/all_to_all | solution.py:517
  43.4 0.2 shard_map.81
  43.6 30.4 %all_to_all.11 = f32[64,1,128]{2,1,0:T(1,128)S(1)} all-to-all(f32[64,1,128]{2,1,0:T(1,128)S(1)} %bitcast.15), channel_id=1, replica_groups=mesh['y'=8,'x'=8,'core'=2,'z'=8] {'y','z'}, dimensions={0} | all-to-all | bytes 65536 | tf_op jit(solution)/shard_map/all_to_all | solution.py:519
  74.0 1.4 %shard_map.82 = (f32[3,2,8,128]{3,2,1,0:T(8,128)}, f32[6,2,8,128]{3,2,1,0:T(8,128)}) custom-call(f32[64,128]{1,0:T(8,128)S(1)} %bitcast.14, f32[4,3,3,16,128]{4,3,2,1,0:T(8,128)S(1)} %get-tuple-element.17.basis, f32[22,8,128]{2,1,0:T(8,128)S(1)} %get-tuple-element.10.own, f32[8,128]{1,0:T(8,128)S(1)} %get-tuple-element.13.table), custom_call_target="tpu_custom_call" | custom-call | flops 100000 | bytes 100000 | tf_op jit(solution)/shard_map/pallas_call | solution.py:521
  (1 shorter events, 0.0 us)
Async XLA Ops:
  1.5 7.2 %collective-permute-start = (f32[11,8,128]{2,1,0:T(8,128)S(1)}, f32[11,8,128]{2,1,0:T(8,128)S(1)}, u32[]{:S(2)}, u32[]{:S(2)}) collective-permute-start(f32[11,8,128]{2,1,0:T(8,128)S(1)} %get-tuple-element.11), channel_id=1, source_target_pairs={{0,1},{2,3},{4,5},{6,7},{1,0},{3,2},{5,4},{7,6},{8,9},{10,11},{12,... | collective-permute-start | bytes 135176 | tf_op jit(solution)/shard_map/ppermute | solution.py:451
  7.3 1.4 %collective-permute-start.1 = (f32[11,8,128]{2,1,0:T(8,128)S(1)}, f32[11,8,128]{2,1,0:T(8,128)S(1)}, u32[]{:S(2)}, u32[]{:S(2)}) collective-permute-start(f32[11,8,128]{2,1,0:T(8,128)S(1)} %get-tuple-element.12), channel_id=1, source_target_pairs={{1,2},{3,4},{5,6},{2,1},{4,3},{6,5},{9,10},{11,12},{13,14},{10,9},... | collective-permute-start | bytes 135176 | tf_op jit(solution)/shard_map/ppermute | solution.py:451
  8.9 6.3 %collective-permute-start.3 = (f32[13,16,128]{2,1,0:T(8,128)S(1)}, f32[13,16,128]{2,1,0:T(8,128)S(1)}, u32[]{:S(2)}, u32[]{:S(2)}) collective-permute-start(f32[13,16,128]{2,1,0:T(8,128)S(1)} %shard_map.78.wide), channel_id=1, source_target_pairs={{16,32},{48,64},{80,96},{112,128},{144,160},{176,192},{208,224},{2... | collective-permute-start | bytes 319496 | tf_op jit(solution)/shard_map/ppermute | solution.py:451
  9.6 7.7 %collective-permute-start.2 = (f32[13,16,128]{2,1,0:T(8,128)S(1)}, f32[13,16,128]{2,1,0:T(8,128)S(1)}, u32[]{:S(2)}, u32[]{:S(2)}) collective-permute-start(f32[13,16,128]{2,1,0:T(8,128)S(1)} %shard_map.78.wide), channel_id=1, source_target_pairs={{0,16},{32,48},{64,80},{96,112},{128,144},{160,176},{192,208},{224... | collective-permute-start | bytes 319496 | tf_op jit(solution)/shard_map/ppermute | solution.py:451
  17.3 14.9 %collective-permute-start.4 = (f32[2,13,16,128]{3,2,1,0:T(8,128)S(1)}, f32[2,13,16,128]{3,2,1,0:T(8,128)S(1)}, u32[]{:S(2)}, u32[]{:S(2)}) collective-permute-start(f32[2,13,16,128]{3,2,1,0:T(8,128)S(1)} %get-tuple-element.15), channel_id=1, source_target_pairs={{0,8},{8,0},{1,9},{9,1},{2,10},{10,2},{3,11},{11,3},{4,12},{12,4},... | collective-permute-start | bytes 638984 | tf_op jit(solution)/shard_map/ppermute | solution.py:504

commit v4 on v3

--- a/solution.py
+++ b/solution.py
@@ -38,9 +38,7 @@
     )
 
 
-def pack_body(
-    odd, load, viscous, material, free, moduli, relax, own, first, second, table, kinds, frees, entries, times, done
-):
+def pack_body(load, viscous, material, free, moduli, relax, own, low, high, table, kinds, frees, entries, times, done):
     pairs = (
         (load, own.at[0:6]),
         (viscous, own.at[6:18]),
@@ -55,7 +53,6 @@
     for copy in copies:
         copy.wait()
     row = lax.broadcasted_iota(jnp.int32, (8, 128), 0)
-    even = jnp.full((8, 128), odd[0], jnp.int32) == 0
     for field in range(FIELDS):
         if field == 9:
             layers = [kinds[layer].astype(F32) - float(CLASSES) for layer in range(2)]
@@ -66,10 +63,8 @@
         if field >= 9:
             for layer in range(2):
                 own[2 * field + layer] = layers[layer]
-        low = jnp.where(row < 4, layers[0], pltpu.roll(layers[1], 4, 0))
-        high = jnp.where(row < 4, pltpu.roll(layers[0], 4, 0), layers[1])
-        first[field] = jnp.where(even, high, low)
-        second[field] = jnp.where(even, low, high)
+        low[field] = jnp.where(row < 4, layers[0], pltpu.roll(layers[1], 4, 0))
+        high[field] = jnp.where(row < 4, pltpu.roll(layers[0], 4, 0), layers[1])
     time = times[...]
     retain = time / (time + 1.0)
     table[...] = jnp.zeros((8, 128), F32)
@@ -84,13 +79,11 @@
     return jnp.take_along_axis(entries, index, axis=1, mode="promise_in_bounds")
 
 
-def widen_body(odd, own, first, second, table, wide):
+def widen_body(own, above, below, table, wide):
     row = lax.broadcasted_iota(jnp.int32, (8, 128), 0)
-    even = jnp.full((8, 128), odd[0], jnp.int32) == 0
 
     def rows(field):
-        upper = jnp.where(even, first[field], second[field])
-        lower = jnp.where(even, second[field], first[field])
+        upper, lower = above[field], below[field]
         halos = (
             jnp.where(row < 4, upper, pltpu.roll(lower, 4, 0)),
             jnp.where(row < 4, pltpu.roll(upper, 4, 0), lower),
@@ -446,6 +439,11 @@
             viscous_next[part, layer] = retain * old + (1.0 - retain) * strain[part][0:8]
 
 
+def shifted(value, axes, count, steps):
+    pairs = [(i, i + steps) for i in range(count) if 0 <= i + steps < count]
+    return lax.ppermute(value, axes, pairs)
+
+
 def swapped(value, axes, count, start):
     lower = [i for i in range(start, count - 1, 2)]
     return lax.ppermute(value, axes, [(i, i + 1) for i in lower] + [(i + 1, i) for i in lower])
@@ -462,11 +460,11 @@
         def parity(axes):
             return (lax.axis_index(axes) % 2).astype(jnp.int32).reshape(1)
 
-        odd_row, odd_chip, core = parity("z"), parity("x"), parity("core")
-        own, first, second, table = call(
+        odd_chip, core = parity("x"), parity("core")
+        own, low, high, table = call(
             pack_body,
             (SDS((22, 8, 128), F32), SDS((11, 8, 128), F32), SDS((11, 8, 128), F32), SDS((8, 128), F32)),
-            7,
+            6,
             scratch=(
                 pltpu.VMEM((2, 8, 128), jnp.int32),
                 pltpu.VMEM((2, 8, 128), jnp.int32),
@@ -475,9 +473,7 @@
                 pltpu.SemaphoreType.DMA((6,)),
             ),
             spec=HBM,
-            scalars=1,
         )(
-            odd_row,
             *(
                 pltpu.with_memory_space_constraint(value, pltpu.HBM)
                 for value in (
@@ -490,9 +486,9 @@
                 )
             )
         )
-        first = swapped(first, ("z",), count_z, 0)
-        second = swapped(second, ("z",), count_z, 1)
-        wide = call(widen_body, SDS((BLOCK, ROWS, 128), F32), 5, scalars=1)(odd_row, own, first, second, table)
+        below = shifted(high, ("z",), count_z, 1)
+        above = shifted(low, ("z",), count_z, -1)
+        wide = call(widen_body, SDS((BLOCK, ROWS, 128), F32), 4)(own, above, below, table)
         first = swapped(wide, ("y", "x"), chips, 0)
         second = swapped(wide, ("y", "x"), chips, 1)
         given, sides = call(
@@ -502,7 +498,7 @@
             scalars=2,
         )(core, odd_chip, wide, first, second)
         taken = lax.ppermute(given, ("core",), [(0, 1), (1, 0)])
-        near, far = 2 * along, across * count_z
+        near, far = along * count_z, 2 * across
         basis, sums = call(
             krylov_body,
             (SDS((ITERS, 3, 3, ROWS, 128), F32), SDS((near, 128), F32)),
@@ -514,9 +510,9 @@
             ),
             flops=20000000,
         )(sides, taken, wide, table)
-        group = lax.all_to_all(sums.reshape(near, 1, 128), ("x", "core"), 0, 0)
+        group = lax.all_to_all(sums.reshape(near, 1, 128), ("x", "z"), 0, 0)
         partial = call(middle_body, SDS((far, 128), F32), 1)(group.reshape(near, 128))
-        everything = lax.all_to_all(partial.reshape(far, 1, 128), ("y", "z"), 0, 0)
+        everything = lax.all_to_all(partial.reshape(far, 1, 128), ("y", "core"), 0, 0)
         return tuple(
             call(final_body, (SDS((3, 2, 8, 128), F32), SDS((6, 2, 8, 128), F32)), 4)(
                 jnp.pad(everything.reshape(far, 128), ((0, -far % 8), (0, 0))), basis, own, table

time: 75.8 us -> 75.3 us (level)
  blocking collectives: 40.2 us -> 38.2 us
  starting transfers between devices: 26.4 us -> 27.7 us
    ppermute x0 -> x2, starting transfers between devices: none -> 7.66 us  [shifted(): return lax.ppermute(value, axes, pairs)]
    ppermute x4 -> x2, starting transfers between devices: 12.6 us -> 6.24 us  [swapped(): lax.ppermute(value, axes, [(i, i + 1) for i in lower] + [(i + 1, i) for i...]
    all_to_all x2, blocking collectives: 40.2 us -> 38.2 us  [the longest x1 22.1 us: shards(): group = lax.all_to_all(sums.reshape(near, 1, 128), ('x', 'z'), 0, 0)]
    ppermute x0 -> x2, waiting for transfers between devices: none -> 1.11 us  [shifted(): return lax.ppermute(value, axes, pairs)]
    ppermute x4 -> x2, waiting for transfers between devices: 2.8 us -> 2.05 us  [swapped(): lax.ppermute(value, axes, [(i, i + 1) for i in lower] + [(i + 1, i) for i...]
where the time goes in v4:
time: 75.3 us; the launch traced here: 75 us
  blocking collectives  38.2 us (51%)
  starting transfers between devices  27.7 us (37%)
  waiting for transfers between devices  4.23 us (6%)
  Pallas kernels  4.14 us (5%)
    all_to_all x1, blocking collectives, shards(): group = lax.all_to_all(sums.reshape(near, 1, 128), ('x', 'z'), 0, 0)  22.1 us
    all_to_all x1, blocking collectives, shards(): lax.all_to_all(partial.reshape(far, 1, 128), ('y', 'core'), 0, 0)  16.1 us
    ppermute x1, starting transfers between devices, shards(): taken = lax.ppermute(given, ('core',), [(0, 1), (1, 0)])  13.8 us
    ppermute x2, starting transfers between devices, shifted(): return lax.ppermute(value, axes, pairs)  7.66 us
    ppermute x2, starting transfers between devices, swapped(): lax.ppermute(value, axes, [(i, i + 1) for i in lower] + [(i + 1, i) for i...  6.24 us
    ppermute x2, waiting for transfers between devices, swapped(): lax.ppermute(value, axes, [(i, i + 1) for i in lower] + [(i + 1, i) for i...  2.05 us
  transfers between devices with their start and end apart: 5, of which 3 were waited for; matrix products, arithmetic and copies ran while one was open for 0% of the time, Pallas kernels for 0%

profile of v4, /device:TPU:1, one launch (start us, length us, event | category | flops | bytes accessed | tf_op | source)
XLA Modules:
  0.0 75.0 jit_solution(11500292196340589770)
XLA Ops:
  0.6 0.9 %shard_map.77 = (f32[22,8,128]{2,1,0:T(8,128)S(1)}, f32[11,8,128]{2,1,0:T(8,128)S(1)}, f32[11,8,128]{2,1,0:T(8,128)S(1)}, f32[8,128]{1,0:T(8,128)S(1)}) custom-call(f32[6,8,128]{2,1,0:T(8,128)} %bitcast.18, f32[12,8,128]{2,1,0:T(8,128)} %bitcast.17, s32[2,8,128]{2,1,0:T(8,128)} %material.1, s32[2,8,128]{2,1,0:T(8,128)} %free.1, f32[3,16]{1,0:T(4,128)} %moduli.1, ...), custom_call_target="tpu_custom_call" | custom-call | flops 100000 | bytes 100000 | tf_op jit(solution)/shard_map/pallas_call | solution.py:464
  1.5 1.3 %collective-permute-start = (f32[11,8,128]{2,1,0:T(8,128)S(1)}, f32[11,8,128]{2,1,0:T(8,128)S(1)}, u32[]{:S(2)}, u32[]{:S(2)}) collective-permute-start(f32[11,8,128]{2,1,0:T(8,128)S(1)} %get-tuple-element.11), channel_id=1, source_target_pairs={{1,0},{2,1},{3,2},{4,3},{5,4},{6,5},{7,6},{9,8},{10,9},{11,10},{12... | collective-permute-start | bytes 135176 | tf_op jit(solution)/shard_map/ppermute | solution.py:444
  2.8 6.4 %collective-permute-start.1 = (f32[11,8,128]{2,1,0:T(8,128)S(1)}, f32[11,8,128]{2,1,0:T(8,128)S(1)}, u32[]{:S(2)}, u32[]{:S(2)}) collective-permute-start(f32[11,8,128]{2,1,0:T(8,128)S(1)} %get-tuple-element.12), channel_id=1, source_target_pairs={{0,1},{1,2},{2,3},{3,4},{4,5},{5,6},{6,7},{8,9},{9,10},{10,11},{11... | collective-permute-start | bytes 135176 | tf_op jit(solution)/shard_map/ppermute | solution.py:444
  9.2 0.0 collective-permute-done.above
  9.2 1.1 %collective-permute-done.1.below = f32[11,8,128]{2,1,0:T(8,128)S(1)} collective-permute-done((f32[11,8,128]{2,1,0:T(8,128)S(1)}, f32[11,8,128]{2,1,0:T(8,128)S(1)}, u32[]{:S(2)}, u32[]{:S(2)}) %collective-permute-start.1) | collective-permute-done | bytes 45088 | tf_op jit(solution)/shard_map/ppermute | solution.py:444
  10.3 0.2 shard_map.78.wide
  10.5 0.7 collective-permute-start.3
  11.2 5.6 %collective-permute-start.2 = (f32[13,16,128]{2,1,0:T(8,128)S(1)}, f32[13,16,128]{2,1,0:T(8,128)S(1)}, u32[]{:S(2)}, u32[]{:S(2)}) collective-permute-start(f32[13,16,128]{2,1,0:T(8,128)S(1)} %shard_map.78.wide), channel_id=1, source_target_pairs={{0,16},{32,48},{64,80},{96,112},{128,144},{160,176},{192,208},{224... | collective-permute-start | bytes 319496 | tf_op jit(solution)/shard_map/ppermute | solution.py:449
  16.8 0.0 collective-permute-done.3.second
  16.8 2.1 %collective-permute-done.2.first = f32[13,16,128]{2,1,0:T(8,128)S(1)} collective-permute-done((f32[13,16,128]{2,1,0:T(8,128)S(1)}, f32[13,16,128]{2,1,0:T(8,128)S(1)}, u32[]{:S(2)}, u32[]{:S(2)}) %collective-permute-start.2) | collective-permute-done | bytes 106528 | tf_op jit(solution)/shard_map/ppermute | solution.py:449
  18.9 13.8 %collective-permute-start.4 = (f32[2,13,16,128]{3,2,1,0:T(8,128)S(1)}, f32[2,13,16,128]{3,2,1,0:T(8,128)S(1)}, u32[]{:S(2)}, u32[]{:S(2)}) collective-permute-start(f32[2,13,16,128]{3,2,1,0:T(8,128)S(1)} %get-tuple-element.15), channel_id=1, source_target_pairs={{0,8},{8,0},{1,9},{9,1},{2,10},{10,2},{3,11},{11,3},{4,12},{12,4},... | collective-permute-start | bytes 638984 | tf_op jit(solution)/shard_map/ppermute | solution.py:500
  32.7 1.1 %collective-permute-done.4.rec = f32[2,13,16,128]{3,2,1,0:T(8,128)S(1)} collective-permute-done((f32[2,13,16,128]{3,2,1,0:T(8,128)S(1)}, f32[2,13,16,128]{3,2,1,0:T(8,128)S(1)}, u32[]{:S(2)}, u32[]{:S(2)}) %collective-permute-start.4) | collective-permute-done | bytes 213024 | tf_op jit(solution)/shard_map/ppermute | solution.py:500
  33.7 1.5 %shard_map.80 = (f32[4,3,3,16,128]{4,3,2,1,0:T(8,128)S(1)}, f32[64,128]{1,0:T(8,128)S(1)}) custom-call(f32[2,13,16,128]{3,2,1,0:T(8,128)S(1)} %get-tuple-element.14.sides, f32[2,13,16,128]{3,2,1,0:T(8,128)S(1)} %collective-permute-done.4.rec, f32[13,16,128]{2,1,0:T(8,128)S(1)} %shard_map.78.wide, f32[8,128]{1,0:T(8,128)S(1)} %get-tuple-element.13.table), custom_call_target="tpu_custom_call" | custom-call | flops 20000000 | bytes 100000 | tf_op jit(solution)/shard_map/pallas_call | solution.py:502
  35.2 22.1 %all_to_all.10 = f32[64,1,128]{2,1,0:T(1,128)S(1)} all-to-all(f32[64,1,128]{2,1,0:T(1,128)S(1)} %bitcast.16), channel_id=1, replica_groups=mesh['y'=8,'x'=8,'core'=2,'z'=8] {'x','z'}, dimensions={0} | all-to-all | bytes 65536 | tf_op jit(solution)/shard_map/all_to_all | solution.py:513
  57.3 0.2 shard_map.81
  57.5 16.1 %all_to_all.11 = f32[16,1,128]{2,1,0:T(1,128)S(1)} all-to-all(f32[16,1,128]{2,1,0:T(1,128)S(1)} %bitcast.15), channel_id=1, replica_groups=mesh['y'=8,'x'=8,'core'=2,'z'=8] {'y','core'}, dimensions={0} | all-to-all | bytes 16384 | tf_op jit(solution)/shard_map/all_to_all | solution.py:515
  73.6 1.3 %shard_map.82 = (f32[3,2,8,128]{3,2,1,0:T(8,128)}, f32[6,2,8,128]{3,2,1,0:T(8,128)}) custom-call(f32[16,128]{1,0:T(8,128)S(1)} %bitcast.14, f32[4,3,3,16,128]{4,3,2,1,0:T(8,128)S(1)} %get-tuple-element.17.basis, f32[22,8,128]{2,1,0:T(8,128)S(1)} %get-tuple-element.10.own, f32[8,128]{1,0:T(8,128)S(1)} %get-tuple-element.13.table), custom_call_target="tpu_custom_call" | custom-call | flops 100000 | bytes 100000 | tf_op jit(solution)/shard_map/pallas_call | solution.py:517
  (1 shorter events, 0.0 us)
Async XLA Ops:
  1.5 7.7 %collective-permute-start = (f32[11,8,128]{2,1,0:T(8,128)S(1)}, f32[11,8,128]{2,1,0:T(8,128)S(1)}, u32[]{:S(2)}, u32[]{:S(2)}) collective-permute-start(f32[11,8,128]{2,1,0:T(8,128)S(1)} %get-tuple-element.11), channel_id=1, source_target_pairs={{1,0},{2,1},{3,2},{4,3},{5,4},{6,5},{7,6},{9,8},{10,9},{11,10},{12... | collective-permute-start | bytes 135176 | tf_op jit(solution)/shard_map/ppermute | solution.py:444
  2.8 7.5 %collective-permute-start.1 = (f32[11,8,128]{2,1,0:T(8,128)S(1)}, f32[11,8,128]{2,1,0:T(8,128)S(1)}, u32[]{:S(2)}, u32[]{:S(2)}) collective-permute-start(f32[11,8,128]{2,1,0:T(8,128)S(1)} %get-tuple-element.12), channel_id=1, source_target_pairs={{0,1},{1,2},{2,3},{3,4},{4,5},{5,6},{6,7},{8,9},{9,10},{10,11},{11... | collective-permute-start | bytes 135176 | tf_op jit(solution)/shard_map/ppermute | solution.py:444
  10.5 6.3 %collective-permute-start.3 = (f32[13,16,128]{2,1,0:T(8,128)S(1)}, f32[13,16,128]{2,1,0:T(8,128)S(1)}, u32[]{:S(2)}, u32[]{:S(2)}) collective-permute-start(f32[13,16,128]{2,1,0:T(8,128)S(1)} %shard_map.78.wide), channel_id=1, source_target_pairs={{16,32},{48,64},{80,96},{112,128},{144,160},{176,192},{208,224},{2... | collective-permute-start | bytes 319496 | tf_op jit(solution)/shard_map/ppermute | solution.py:449
  11.2 7.7 %collective-permute-start.2 = (f32[13,16,128]{2,1,0:T(8,128)S(1)}, f32[13,16,128]{2,1,0:T(8,128)S(1)}, u32[]{:S(2)}, u32[]{:S(2)}) collective-permute-start(f32[13,16,128]{2,1,0:T(8,128)S(1)} %shard_map.78.wide), channel_id=1, source_target_pairs={{0,16},{32,48},{64,80},{96,112},{128,144},{160,176},{192,208},{224... | collective-permute-start | bytes 319496 | tf_op jit(solution)/shard_map/ppermute | solution.py:449
  18.9 14.8 %collective-permute-start.4 = (f32[2,13,16,128]{3,2,1,0:T(8,128)S(1)}, f32[2,13,16,128]{3,2,1,0:T(8,128)S(1)}, u32[]{:S(2)}, u32[]{:S(2)}) collective-permute-start(f32[2,13,16,128]{3,2,1,0:T(8,128)S(1)} %get-tuple-element.15), channel_id=1, source_target_pairs={{0,8},{8,0},{1,9},{9,1},{2,10},{10,2},{3,11},{11,3},{4,12},{12,4},... | collective-permute-start | bytes 638984 | tf_op jit(solution)/shard_map/ppermute | solution.py:500

commit v5 on v4

--- a/solution.py
+++ b/solution.py
@@ -114,26 +114,26 @@
         wide[3 * comp + 2] = fields[comp][1] + node_force(pending[comp])
 
 
-def choose_body(core, odd, wide, first, second, given, sides):
+def order_body(core, odd, chip_first, chip_second, own_chip, next_chip, sides, rec):
     @pl.when(odd[0] == 0)
     def _():
-        sides[0] = second[...]
-        sides[1] = first[...]
+        sides[0] = chip_second[...]
+        sides[1] = chip_first[...]
 
     @pl.when(odd[0] != 0)
     def _():
-        sides[0] = first[...]
-        sides[1] = second[...]
+        sides[0] = chip_first[...]
+        sides[1] = chip_second[...]
 
     @pl.when(core[0] == 0)
     def _():
-        given[0] = wide[...]
-        given[1] = sides[1]
+        rec[0] = next_chip[...]
+        rec[1] = own_chip[...]
 
     @pl.when(core[0] != 0)
     def _():
-        given[0] = sides[0]
-        given[1] = wide[...]
+        rec[0] = own_chip[...]
+        rec[1] = next_chip[...]
 
 
 def iota(axis, shape=(ROWS, 128)):
@@ -491,13 +491,14 @@
         wide = call(widen_body, SDS((BLOCK, ROWS, 128), F32), 4)(own, above, below, table)
         first = swapped(wide, ("y", "x"), chips, 0)
         second = swapped(wide, ("y", "x"), chips, 1)
-        given, sides = call(
-            choose_body,
+        own_chip = swapped(wide, ("y", "x", "core"), count_x, 0)
+        next_chip = swapped(wide, ("y", "x", "core"), count_x, 1)
+        sides, taken = call(
+            order_body,
             (SDS((2, BLOCK, ROWS, 128), F32), SDS((2, BLOCK, ROWS, 128), F32)),
-            5,
+            6,
             scalars=2,
-        )(core, odd_chip, wide, first, second)
-        taken = lax.ppermute(given, ("core",), [(0, 1), (1, 0)])
+        )(core, odd_chip, first, second, own_chip, next_chip)
         near, far = along * count_z, 2 * across
         basis, sums = call(
             krylov_body,

time: 75.3 us -> 78.6 us (1.044)
  blocking collectives: 38.2 us -> 42 us
  starting transfers between devices: 27.7 us -> 25.7 us
  waiting for transfers between devices: 4.23 us -> 5.63 us
    ppermute x1 -> x0, starting transfers between devices: 13.8 us -> none  [shards(): taken = lax.ppermute(given, ('core',), [(0, 1), (1, 0)])]
    ppermute x2 -> x4, starting transfers between devices: 6.24 us -> 18.1 us  [swapped(): lax.ppermute(value, axes, [(i, i + 1) for i in lower] + [(i + 1, i) for i...]
    ppermute x2 -> x4, waiting for transfers between devices: 2.05 us -> 4.51 us  [swapped(): lax.ppermute(value, axes, [(i, i + 1) for i in lower] + [(i + 1, i) for i...]
    all_to_all x1, blocking collectives: 22.1 us -> 24.3 us  [shards(): group = lax.all_to_all(sums.reshape(near, 1, 128), ('x', 'z'), 0, 0)]
    all_to_all x1, blocking collectives: 16.1 us -> 17.7 us  [shards(): lax.all_to_all(partial.reshape(far, 1, 128), ('y', 'core'), 0, 0)]
    ppermute x1 -> x0, waiting for transfers between devices: 1.07 us -> none  [shards(): taken = lax.ppermute(given, ('core',), [(0, 1), (1, 0)])]
  transfers between devices with their start and end apart: 5 -> 6, of which waited for: 3 -> 2; matrix products, arithmetic and copies ran while one was open for 0% -> 0% of each run, Pallas kernels for 0% -> 0%
where the time goes in v5:
time: 78.6 us; the launch traced here: 78.3 us
  blocking collectives  42 us (53%)
  starting transfers between devices  25.7 us (33%)
  waiting for transfers between devices  5.63 us (7%)
  Pallas kernels  4.14 us (5%)
    all_to_all x1, blocking collectives, shards(): group = lax.all_to_all(sums.reshape(near, 1, 128), ('x', 'z'), 0, 0)  24.3 us
    ppermute x4, starting transfers between devices, swapped(): lax.ppermute(value, axes, [(i, i + 1) for i in lower] + [(i + 1, i) for i...  18.1 us
    all_to_all x1, blocking collectives, shards(): lax.all_to_all(partial.reshape(far, 1, 128), ('y', 'core'), 0, 0)  17.7 us
    ppermute x2, starting transfers between devices, shifted(): return lax.ppermute(value, axes, pairs)  7.66 us
    ppermute x4, waiting for transfers between devices, swapped(): lax.ppermute(value, axes, [(i, i + 1) for i in lower] + [(i + 1, i) for i...  4.51 us
  transfers between devices with their start and end apart: 6, of which 2 were waited for; matrix products, arithmetic and copies ran while one was open for 0% of the time, Pallas kernels for 0%

profile of v5, /device:TPU:1, one launch (start us, length us, event | category | flops | bytes accessed | tf_op | source)
XLA Modules:
  0.0 78.3 jit_solution(3889626354760695597)
XLA Ops:
  0.6 0.9 %shard_map.77 = (f32[22,8,128]{2,1,0:T(8,128)S(1)}, f32[11,8,128]{2,1,0:T(8,128)S(1)}, f32[11,8,128]{2,1,0:T(8,128)S(1)}, f32[8,128]{1,0:T(8,128)S(1)}) custom-call(f32[6,8,128]{2,1,0:T(8,128)} %bitcast.18, f32[12,8,128]{2,1,0:T(8,128)} %bitcast.17, s32[2,8,128]{2,1,0:T(8,128)} %material.1, s32[2,8,128]{2,1,0:T(8,128)} %free.1, f32[3,16]{1,0:T(4,128)} %moduli.1, ...), custom_call_target="tpu_custom_call" | custom-call | flops 100000 | bytes 100000 | tf_op jit(solution)/shard_map/pallas_call | solution.py:464
  1.5 1.3 %collective-permute-start = (f32[11,8,128]{2,1,0:T(8,128)S(1)}, f32[11,8,128]{2,1,0:T(8,128)S(1)}, u32[]{:S(2)}, u32[]{:S(2)}) collective-permute-start(f32[11,8,128]{2,1,0:T(8,128)S(1)} %get-tuple-element.11), channel_id=1, source_target_pairs={{1,0},{2,1},{3,2},{4,3},{5,4},{6,5},{7,6},{9,8},{10,9},{11,10},{12... | collective-permute-start | bytes 135176 | tf_op jit(solution)/shard_map/ppermute | solution.py:444
  2.8 6.4 %collective-permute-start.1 = (f32[11,8,128]{2,1,0:T(8,128)S(1)}, f32[11,8,128]{2,1,0:T(8,128)S(1)}, u32[]{:S(2)}, u32[]{:S(2)}) collective-permute-start(f32[11,8,128]{2,1,0:T(8,128)S(1)} %get-tuple-element.12), channel_id=1, source_target_pairs={{0,1},{1,2},{2,3},{3,4},{4,5},{5,6},{6,7},{8,9},{9,10},{10,11},{11... | collective-permute-start | bytes 135176 | tf_op jit(solution)/shard_map/ppermute | solution.py:444
  9.2 0.0 collective-permute-done.above
  9.2 1.1 %collective-permute-done.1.below = f32[11,8,128]{2,1,0:T(8,128)S(1)} collective-permute-done((f32[11,8,128]{2,1,0:T(8,128)S(1)}, f32[11,8,128]{2,1,0:T(8,128)S(1)}, u32[]{:S(2)}, u32[]{:S(2)}) %collective-permute-start.1) | collective-permute-done | bytes 45088 | tf_op jit(solution)/shard_map/ppermute | solution.py:444
  10.3 0.2 shard_map.78.wide
  10.5 4.5 %collective-permute-start.5 = (f32[13,16,128]{2,1,0:T(8,128)S(1)}, f32[13,16,128]{2,1,0:T(8,128)S(1)}, u32[]{:S(2)}, u32[]{:S(2)}) collective-permute-start(f32[13,16,128]{2,1,0:T(8,128)S(1)} %shard_map.78.wide), channel_id=1, source_target_pairs={{8,16},{24,32},{40,48},{56,64},{72,80},{88,96},{104,112},{120,128}... | collective-permute-start | bytes 319496 | tf_op jit(solution)/shard_map/ppermute | solution.py:449
  15.1 11.0 %collective-permute-start.4 = (f32[13,16,128]{2,1,0:T(8,128)S(1)}, f32[13,16,128]{2,1,0:T(8,128)S(1)}, u32[]{:S(2)}, u32[]{:S(2)}) collective-permute-start(f32[13,16,128]{2,1,0:T(8,128)S(1)} %shard_map.78.wide), channel_id=1, source_target_pairs={{0,8},{16,24},{32,40},{48,56},{64,72},{80,88},{96,104},{112,120},{... | collective-permute-start | bytes 319496 | tf_op jit(solution)/shard_map/ppermute | solution.py:449
  26.0 0.7 collective-permute-start.3
  26.7 1.9 %collective-permute-start.2 = (f32[13,16,128]{2,1,0:T(8,128)S(1)}, f32[13,16,128]{2,1,0:T(8,128)S(1)}, u32[]{:S(2)}, u32[]{:S(2)}) collective-permute-start(f32[13,16,128]{2,1,0:T(8,128)S(1)} %shard_map.78.wide), channel_id=1, source_target_pairs={{0,16},{32,48},{64,80},{96,112},{128,144},{160,176},{192,208},{224... | collective-permute-start | bytes 319496 | tf_op jit(solution)/shard_map/ppermute | solution.py:449
  28.6 0.0 collective-permute-done.5.next_chip
  28.7 0.0 collective-permute-done.4.own_chip
  28.7 0.0 collective-permute-done.3.chip_second
  28.7 4.5 %collective-permute-done.2.chip_first = f32[13,16,128]{2,1,0:T(8,128)S(1)} collective-permute-done((f32[13,16,128]{2,1,0:T(8,128)S(1)}, f32[13,16,128]{2,1,0:T(8,128)S(1)}, u32[]{:S(2)}, u32[]{:S(2)}) %collective-permute-start.2) | collective-permute-done | bytes 106528 | tf_op jit(solution)/shard_map/ppermute | solution.py:449
  33.2 1.5 %shard_map.80 = (f32[4,3,3,16,128]{4,3,2,1,0:T(8,128)S(1)}, f32[64,128]{1,0:T(8,128)S(1)}) custom-call(f32[2,13,16,128]{3,2,1,0:T(8,128)S(1)} %get-tuple-element.14.sides, f32[2,13,16,128]{3,2,1,0:T(8,128)S(1)} %get-tuple-element.15.rec, f32[13,16,128]{2,1,0:T(8,128)S(1)} %shard_map.78.wide, f32[8,128]{1,0:T(8,128)S(1)} %get-tuple-element.13.table), custom_call_target="tpu_custom_call" | custom-call | flops 20000000 | bytes 100000 | tf_op jit(solution)/shard_map/pallas_call | solution.py:503
  34.7 24.3 %all_to_all.10 = f32[64,1,128]{2,1,0:T(1,128)S(1)} all-to-all(f32[64,1,128]{2,1,0:T(1,128)S(1)} %bitcast.16), channel_id=1, replica_groups=mesh['y'=8,'x'=8,'core'=2,'z'=8] {'x','z'}, dimensions={0} | all-to-all | bytes 65536 | tf_op jit(solution)/shard_map/all_to_all | solution.py:514
  59.0 0.2 shard_map.81
  59.2 17.7 %all_to_all.11 = f32[16,1,128]{2,1,0:T(1,128)S(1)} all-to-all(f32[16,1,128]{2,1,0:T(1,128)S(1)} %bitcast.15), channel_id=1, replica_groups=mesh['y'=8,'x'=8,'core'=2,'z'=8] {'y','core'}, dimensions={0} | all-to-all | bytes 16384 | tf_op jit(solution)/shard_map/all_to_all | solution.py:516
  76.9 1.3 %shard_map.82 = (f32[3,2,8,128]{3,2,1,0:T(8,128)}, f32[6,2,8,128]{3,2,1,0:T(8,128)}) custom-call(f32[16,128]{1,0:T(8,128)S(1)} %bitcast.14, f32[4,3,3,16,128]{4,3,2,1,0:T(8,128)S(1)} %get-tuple-element.17.basis, f32[22,8,128]{2,1,0:T(8,128)S(1)} %get-tuple-element.10.own, f32[8,128]{1,0:T(8,128)S(1)} %get-tuple-element.13.table), custom_call_target="tpu_custom_call" | custom-call | flops 100000 | bytes 100000 | tf_op jit(solution)/shard_map/pallas_call | solution.py:518
  (1 shorter events, 0.0 us)
Async XLA Ops:
  1.5 7.7 %collective-permute-start = (f32[11,8,128]{2,1,0:T(8,128)S(1)}, f32[11,8,128]{2,1,0:T(8,128)S(1)}, u32[]{:S(2)}, u32[]{:S(2)}) collective-permute-start(f32[11,8,128]{2,1,0:T(8,128)S(1)} %get-tuple-element.11), channel_id=1, source_target_pairs={{1,0},{2,1},{3,2},{4,3},{5,4},{6,5},{7,6},{9,8},{10,9},{11,10},{12... | collective-permute-start | bytes 135176 | tf_op jit(solution)/shard_map/ppermute | solution.py:444
  2.8 7.5 %collective-permute-start.1 = (f32[11,8,128]{2,1,0:T(8,128)S(1)}, f32[11,8,128]{2,1,0:T(8,128)S(1)}, u32[]{:S(2)}, u32[]{:S(2)}) collective-permute-start(f32[11,8,128]{2,1,0:T(8,128)S(1)} %get-tuple-element.12), channel_id=1, source_target_pairs={{0,1},{1,2},{2,3},{3,4},{4,5},{5,6},{6,7},{8,9},{9,10},{10,11},{11... | collective-permute-start | bytes 135176 | tf_op jit(solution)/shard_map/ppermute | solution.py:444
  10.5 18.1 %collective-permute-start.5 = (f32[13,16,128]{2,1,0:T(8,128)S(1)}, f32[13,16,128]{2,1,0:T(8,128)S(1)}, u32[]{:S(2)}, u32[]{:S(2)}) collective-permute-start(f32[13,16,128]{2,1,0:T(8,128)S(1)} %shard_map.78.wide), channel_id=1, source_target_pairs={{8,16},{24,32},{40,48},{56,64},{72,80},{88,96},{104,112},{120,128}... | collective-permute-start | bytes 319496 | tf_op jit(solution)/shard_map/ppermute | solution.py:449
  15.1 13.6 %collective-permute-start.4 = (f32[13,16,128]{2,1,0:T(8,128)S(1)}, f32[13,16,128]{2,1,0:T(8,128)S(1)}, u32[]{:S(2)}, u32[]{:S(2)}) collective-permute-start(f32[13,16,128]{2,1,0:T(8,128)S(1)} %shard_map.78.wide), channel_id=1, source_target_pairs={{0,8},{16,24},{32,40},{48,56},{64,72},{80,88},{96,104},{112,120},{... | collective-permute-start | bytes 319496 | tf_op jit(solution)/shard_map/ppermute | solution.py:449
  26.0 2.6 %collective-permute-start.3 = (f32[13,16,128]{2,1,0:T(8,128)S(1)}, f32[13,16,128]{2,1,0:T(8,128)S(1)}, u32[]{:S(2)}, u32[]{:S(2)}) collective-permute-start(f32[13,16,128]{2,1,0:T(8,128)S(1)} %shard_map.78.wide), channel_id=1, source_target_pairs={{16,32},{48,64},{80,96},{112,128},{144,160},{176,192},{208,224},{2... | collective-permute-start | bytes 319496 | tf_op jit(solution)/shard_map/ppermute | solution.py:449
  26.7 6.5 %collective-permute-start.2 = (f32[13,16,128]{2,1,0:T(8,128)S(1)}, f32[13,16,128]{2,1,0:T(8,128)S(1)}, u32[]{:S(2)}, u32[]{:S(2)}) collective-permute-start(f32[13,16,128]{2,1,0:T(8,128)S(1)} %shard_map.78.wide), channel_id=1, source_target_pairs={{0,16},{32,48},{64,80},{96,112},{128,144},{160,176},{192,208},{224... | collective-permute-start | bytes 319496 | tf_op jit(solution)/shard_map/ppermute | solution.py:449

commit v6 on v4

--- a/solution.py
+++ b/solution.py
@@ -10,8 +10,8 @@
 ITERS = 4
 ROWS = 16
 LAYERS = 10
-FIELDS = 11
 BLOCK = 13
+HALF = 7
 CLASSES = 16
 MOMENTS = 2 * ITERS
 SCALE = 1.0 / 32.0
@@ -38,10 +38,17 @@
     )
 
 
-def pack_body(load, viscous, material, free, moduli, relax, own, low, high, table, kinds, frees, entries, times, done):
+def pick(table, row, index):
+    entries = jnp.broadcast_to(table[row : row + 1], index.shape)
+    return jnp.take_along_axis(entries, index, axis=1, mode="promise_in_bounds")
+
+
+def pack_body(
+    load, viscous, material, free, moduli, relax, own, part, low, high, table, loads, kinds, frees, entries, times, done
+):
     pairs = (
-        (load, own.at[0:6]),
-        (viscous, own.at[6:18]),
+        (load, loads),
+        (viscous, own.at[0:12]),
         (material, kinds),
         (free, frees),
         (moduli, entries),
@@ -52,19 +59,6 @@
         copy.start()
     for copy in copies:
         copy.wait()
-    row = lax.broadcasted_iota(jnp.int32, (8, 128), 0)
-    for field in range(FIELDS):
-        if field == 9:
-            layers = [kinds[layer].astype(F32) - float(CLASSES) for layer in range(2)]
-        elif field == 10:
-            layers = [frees[layer].astype(F32) for layer in range(2)]
-        else:
-            layers = [own[2 * field + layer] for layer in range(2)]
-        if field >= 9:
-            for layer in range(2):
-                own[2 * field + layer] = layers[layer]
-        low[field] = jnp.where(row < 4, layers[0], pltpu.roll(layers[1], 4, 0))
-        high[field] = jnp.where(row < 4, pltpu.roll(layers[0], 4, 0), layers[1])
     time = times[...]
     retain = time / (time + 1.0)
     table[...] = jnp.zeros((8, 128), F32)
@@ -72,33 +66,19 @@
     table[1:2, 0:CLASSES] = entries[1:2] * (1.0 / 16.0)
     table[2:3, 0:CLASSES] = (entries[2:3] * retain) * (1.0 / 16.0)
     table[3:4, 0:CLASSES] = retain
-
-
-def pick(table, row, index):
-    entries = jnp.broadcast_to(table[row : row + 1], index.shape)
-    return jnp.take_along_axis(entries, index, axis=1, mode="promise_in_bounds")
-
-
-def widen_body(own, above, below, table, wide):
-    row = lax.broadcasted_iota(jnp.int32, (8, 128), 0)
-
-    def rows(field):
-        upper, lower = above[field], below[field]
-        halos = (
-            jnp.where(row < 4, upper, pltpu.roll(lower, 4, 0)),
-            jnp.where(row < 4, pltpu.roll(upper, 4, 0), lower),
-        )
-        return [jnp.concatenate([own[2 * field + layer], halos[layer]], axis=0) for layer in range(2)]
-
-    fields = [rows(field) for field in range(FIELDS)]
-    for layer in range(2):
-        wide[9 + layer] = fields[9][layer]
-        wide[11 + layer] = fields[10][layer]
+    nothing = jnp.zeros((8, 128), F32)
+
+    def tall(tile):
+        return jnp.concatenate([tile, nothing], axis=0)
+
     pending = None
     for layer in range(2):
-        index = fields[9][layer].astype(jnp.int32) + CLASSES
-        factor = 8.0 * pick(table, 2, index)
-        xx, yy, zz, yz, xz, xy = (factor * fields[3 + part][layer] for part in range(6))
+        kind = kinds[layer]
+        own[12 + layer] = kind.astype(F32) - float(CLASSES)
+        part[9 + layer] = tall(own[12 + layer])
+        part[11 + layer] = tall(frees[layer].astype(F32))
+        factor = 8.0 * pick(table, 2, kind)
+        xx, yy, zz, yz, xz, xy = (tall(factor * own[2 * number + layer]) for number in range(6))
         forces = (
             {"dss": xx, "ssd": xz, "sds": xy},
             {"sds": yy, "ssd": yz, "dss": xy},
@@ -108,10 +88,41 @@
         pairs = lower if pending is None else merged(pending, lower)
         for comp in range(3):
             force = node_force(pairs[comp])
-            wide[3 * comp + layer] = force if layer == 0 else fields[comp][0] + force
+            part[3 * comp + layer] = force if layer == 0 else tall(loads[2 * comp]) + force
         pending = upper
     for comp in range(3):
-        wide[3 * comp + 2] = fields[comp][1] + node_force(pending[comp])
+        part[3 * comp + 2] = tall(loads[2 * comp + 1]) + node_force(pending[comp])
+    row = lax.broadcasted_iota(jnp.int32, (8, 128), 0)
+    for pair in range(HALF):
+        firsts, lasts = [], []
+        for k in (2 * pair, 2 * pair + 1):
+            if k >= BLOCK:
+                firsts.append(nothing)
+                lasts.append(nothing)
+                continue
+            tile = part[k]
+            firsts.append(pltpu.roll(tile, 1, 0)[0:8] if k < 9 else tile[0:8])
+            lasts.append(tile[0:8])
+        low[pair] = jnp.where(row < 4, firsts[0], pltpu.roll(firsts[1], 4, 0))
+        high[pair] = jnp.where(row < 4, pltpu.roll(lasts[0], 4, 0), lasts[1])
+
+
+def widen_body(part, above, below, wide):
+    row = lax.broadcasted_iota(jnp.int32, (8, 128), 0)
+    nothing = jnp.zeros((8, 128), F32)
+    for k in range(BLOCK):
+        upper, lower = above[k // 2], below[k // 2]
+        if k % 2 == 0:
+            lower = pltpu.roll(lower, 4, 0)
+        else:
+            upper = pltpu.roll(upper, 4, 0)
+        if k < 9:
+            first = jnp.concatenate([jnp.where(row < 4, upper, 0.0), nothing], axis=0)
+            last = jnp.concatenate([nothing, jnp.where(row < 4, 0.0, lower)], axis=0)
+            wide[k] = part[k] + (pltpu.roll(first, 7, 0) + last)
+        else:
+            wide[k, 0:8] = part[k, 0:8]
+            wide[k, 8:16] = jnp.where(row < 4, upper, lower)
 
 
 def choose_body(core, odd, wide, first, second, given, sides):
@@ -431,11 +442,11 @@
             0.125 * (w["dss"] + u["ssd"]),
             0.125 * (v["dss"] + u["sds"]),
         )
-        index = own[18 + layer].astype(jnp.int32) + CLASSES
+        index = own[12 + layer].astype(jnp.int32) + CLASSES
         entries = jnp.broadcast_to(table[3:4], (8, 128))
         retain = jnp.take_along_axis(entries, index, axis=1, mode="promise_in_bounds")
         for part in range(6):
-            old = own[6 + 2 * part + layer]
+            old = own[2 * part + layer]
             viscous_next[part, layer] = retain * old + (1.0 - retain) * strain[part][0:8]
 
 
@@ -461,11 +472,18 @@
             return (lax.axis_index(axes) % 2).astype(jnp.int32).reshape(1)
 
         odd_chip, core = parity("x"), parity("core")
-        own, low, high, table = call(
+        own, part, low, high, table = call(
             pack_body,
-            (SDS((22, 8, 128), F32), SDS((11, 8, 128), F32), SDS((11, 8, 128), F32), SDS((8, 128), F32)),
+            (
+                SDS((14, 8, 128), F32),
+                SDS((BLOCK, ROWS, 128), F32),
+                SDS((HALF, 8, 128), F32),
+                SDS((HALF, 8, 128), F32),
+                SDS((8, 128), F32),
+            ),
             6,
             scratch=(
+                pltpu.VMEM((6, 8, 128), F32),
                 pltpu.VMEM((2, 8, 128), jnp.int32),
                 pltpu.VMEM((2, 8, 128), jnp.int32),
                 pltpu.VMEM((3, CLASSES), F32),
@@ -488,7 +506,7 @@
         )
         below = shifted(high, ("z",), count_z, 1)
         above = shifted(low, ("z",), count_z, -1)
-        wide = call(widen_body, SDS((BLOCK, ROWS, 128), F32), 4)(own, above, below, table)
+        wide = call(widen_body, SDS((BLOCK, ROWS, 128), F32), 3)(part, above, below)
         first = swapped(wide, ("y", "x"), chips, 0)
         second = swapped(wide, ("y", "x"), chips, 1)
         given, sides = call(

time: 75.3 us -> 75.1 us (level)
  no operation moved by 1% of the time
where the time goes in v6:
time: 75.1 us; the launch traced here: 74.8 us
  blocking collectives  38.2 us (51%)
  starting transfers between devices  27.7 us (37%)
  Pallas kernels  4.13 us (5%)
  waiting for transfers between devices  4.08 us (5%)
    all_to_all x1, blocking collectives, shards(): group = lax.all_to_all(sums.reshape(near, 1, 128), ('x', 'z'), 0, 0)  22 us
    all_to_all x1, blocking collectives, shards(): lax.all_to_all(partial.reshape(far, 1, 128), ('y', 'core'), 0, 0)  16.1 us
    ppermute x1, starting transfers between devices, shards(): taken = lax.ppermute(given, ('core',), [(0, 1), (1, 0)])  13.8 us
    ppermute x2, starting transfers between devices, shifted(): return lax.ppermute(value, axes, pairs)  7.66 us
    ppermute x2, starting transfers between devices, swapped(): lax.ppermute(value, axes, [(i, i + 1) for i in lower] + [(i + 1, i) for i...  6.24 us
    ppermute x2, waiting for transfers between devices, swapped(): lax.ppermute(value, axes, [(i, i + 1) for i in lower] + [(i + 1, i) for i...  2.05 us
  transfers between devices with their start and end apart: 5, of which 3 were waited for; matrix products, arithmetic and copies ran while one was open for 0% of the time, Pallas kernels for 0%

profile of v6, /device:TPU:1, one launch (start us, length us, event | category | flops | bytes accessed | tf_op | source)
XLA Modules:
  0.0 74.8 jit_solution(13936493568296977412)
XLA Ops:
  0.6 1.1 %shard_map.77 = (f32[14,8,128]{2,1,0:T(8,128)S(1)}, f32[13,16,128]{2,1,0:T(8,128)S(1)}, f32[7,8,128]{2,1,0:T(8,128)S(1)}, f32[7,8,128]{2,1,0:T(8,128)S(1)}, f32[8,128]{1,0:T(8,128)S(1)}) custom-call(f32[6,8,128]{2,1,0:T(8,128)} %bitcast.18, f32[12,8,128]{2,1,0:T(8,128)} %bitcast.17, s32[2,8,128]{2,1,0:T(8,128)} %material.1, s32[2,8,128]{2,1,0:T(8,128)} %free.1, ...), custom_call_target="tpu_custom_call" | custom-call | flops 100000 | bytes 100000 | tf_op jit(solution)/shard_map/pallas_call | solution.py:475
  1.7 1.3 %collective-permute-start = (f32[7,8,128]{2,1,0:T(8,128)S(1)}, f32[7,8,128]{2,1,0:T(8,128)S(1)}, u32[]{:S(2)}, u32[]{:S(2)}) collective-permute-start(f32[7,8,128]{2,1,0:T(8,128)S(1)} %get-tuple-element.12), channel_id=1, source_target_pairs={{1,0},{2,1},{3,2},{4,3},{5,4},{6,5},{7,6},{9,8},{10,9},{11,10},{12... | collective-permute-start | bytes 86024 | tf_op jit(solution)/shard_map/ppermute | solution.py:455
  3.0 6.4 %collective-permute-start.1 = (f32[7,8,128]{2,1,0:T(8,128)S(1)}, f32[7,8,128]{2,1,0:T(8,128)S(1)}, u32[]{:S(2)}, u32[]{:S(2)}) collective-permute-start(f32[7,8,128]{2,1,0:T(8,128)S(1)} %get-tuple-element.13), channel_id=1, source_target_pairs={{0,1},{1,2},{2,3},{3,4},{4,5},{5,6},{6,7},{8,9},{9,10},{10,11},{11... | collective-permute-start | bytes 86024 | tf_op jit(solution)/shard_map/ppermute | solution.py:455
  9.4 0.0 collective-permute-done.above
  9.4 1.0 %collective-permute-done.1.below = f32[7,8,128]{2,1,0:T(8,128)S(1)} collective-permute-done((f32[7,8,128]{2,1,0:T(8,128)S(1)}, f32[7,8,128]{2,1,0:T(8,128)S(1)}, u32[]{:S(2)}, u32[]{:S(2)}) %collective-permute-start.1) | collective-permute-done | bytes 28704 | tf_op jit(solution)/shard_map/ppermute | solution.py:455
  10.4 0.7 collective-permute-start.3
  11.0 5.6 %collective-permute-start.2 = (f32[13,16,128]{2,1,0:T(8,128)S(1)}, f32[13,16,128]{2,1,0:T(8,128)S(1)}, u32[]{:S(2)}, u32[]{:S(2)}) collective-permute-start(f32[13,16,128]{2,1,0:T(8,128)S(1)} %shard_map.78.wide), channel_id=1, source_target_pairs={{0,16},{32,48},{64,80},{96,112},{128,144},{160,176},{192,208},{224... | collective-permute-start | bytes 319496 | tf_op jit(solution)/shard_map/ppermute | solution.py:460
  16.6 0.0 collective-permute-done.3.second
  16.6 2.1 %collective-permute-done.2.first = f32[13,16,128]{2,1,0:T(8,128)S(1)} collective-permute-done((f32[13,16,128]{2,1,0:T(8,128)S(1)}, f32[13,16,128]{2,1,0:T(8,128)S(1)}, u32[]{:S(2)}, u32[]{:S(2)}) %collective-permute-start.2) | collective-permute-done | bytes 106528 | tf_op jit(solution)/shard_map/ppermute | solution.py:460
  18.7 13.8 %collective-permute-start.4 = (f32[2,13,16,128]{3,2,1,0:T(8,128)S(1)}, f32[2,13,16,128]{3,2,1,0:T(8,128)S(1)}, u32[]{:S(2)}, u32[]{:S(2)}) collective-permute-start(f32[2,13,16,128]{3,2,1,0:T(8,128)S(1)} %get-tuple-element.15), channel_id=1, source_target_pairs={{0,8},{8,0},{1,9},{9,1},{2,10},{10,2},{3,11},{11,3},{4,12},{12,4},... | collective-permute-start | bytes 638984 | tf_op jit(solution)/shard_map/ppermute | solution.py:518
  32.5 1.1 %collective-permute-done.4.rec = f32[2,13,16,128]{3,2,1,0:T(8,128)S(1)} collective-permute-done((f32[2,13,16,128]{3,2,1,0:T(8,128)S(1)}, f32[2,13,16,128]{3,2,1,0:T(8,128)S(1)}, u32[]{:S(2)}, u32[]{:S(2)}) %collective-permute-start.4) | collective-permute-done | bytes 213024 | tf_op jit(solution)/shard_map/ppermute | solution.py:518
  33.6 1.5 %shard_map.80 = (f32[4,3,3,16,128]{4,3,2,1,0:T(8,128)S(1)}, f32[64,128]{1,0:T(8,128)S(1)}) custom-call(f32[2,13,16,128]{3,2,1,0:T(8,128)S(1)} %get-tuple-element.14.sides, f32[2,13,16,128]{3,2,1,0:T(8,128)S(1)} %collective-permute-done.4.rec, f32[13,16,128]{2,1,0:T(8,128)S(1)} %shard_map.78.wide, f32[8,128]{1,0:T(8,128)S(1)} %get-tuple-element.16.table), custom_call_target="tpu_custom_call" | custom-call | flops 20000000 | bytes 100000 | tf_op jit(solution)/shard_map/pallas_call | solution.py:520
  35.1 22.0 %all_to_all.10 = f32[64,1,128]{2,1,0:T(1,128)S(1)} all-to-all(f32[64,1,128]{2,1,0:T(1,128)S(1)} %bitcast.16), channel_id=1, replica_groups=mesh['y'=8,'x'=8,'core'=2,'z'=8] {'x','z'}, dimensions={0} | all-to-all | bytes 65536 | tf_op jit(solution)/shard_map/all_to_all | solution.py:531
  57.1 0.2 shard_map.81
  57.3 16.1 %all_to_all.11 = f32[16,1,128]{2,1,0:T(1,128)S(1)} all-to-all(f32[16,1,128]{2,1,0:T(1,128)S(1)} %bitcast.15), channel_id=1, replica_groups=mesh['y'=8,'x'=8,'core'=2,'z'=8] {'y','core'}, dimensions={0} | all-to-all | bytes 16384 | tf_op jit(solution)/shard_map/all_to_all | solution.py:533
  73.4 1.3 %shard_map.82 = (f32[3,2,8,128]{3,2,1,0:T(8,128)}, f32[6,2,8,128]{3,2,1,0:T(8,128)}) custom-call(f32[16,128]{1,0:T(8,128)S(1)} %bitcast.14, f32[4,3,3,16,128]{4,3,2,1,0:T(8,128)S(1)} %get-tuple-element.18.basis, f32[14,8,128]{2,1,0:T(8,128)S(1)} %get-tuple-element.19.own, f32[8,128]{1,0:T(8,128)S(1)} %get-tuple-element.16.table), custom_call_target="tpu_custom_call" | custom-call | flops 100000 | bytes 100000 | tf_op jit(solution)/shard_map/pallas_call | solution.py:535
  (2 shorter events, 0.1 us)
Async XLA Ops:
  1.7 7.7 %collective-permute-start = (f32[7,8,128]{2,1,0:T(8,128)S(1)}, f32[7,8,128]{2,1,0:T(8,128)S(1)}, u32[]{:S(2)}, u32[]{:S(2)}) collective-permute-start(f32[7,8,128]{2,1,0:T(8,128)S(1)} %get-tuple-element.12), channel_id=1, source_target_pairs={{1,0},{2,1},{3,2},{4,3},{5,4},{6,5},{7,6},{9,8},{10,9},{11,10},{12... | collective-permute-start | bytes 86024 | tf_op jit(solution)/shard_map/ppermute | solution.py:455
  3.0 7.3 %collective-permute-start.1 = (f32[7,8,128]{2,1,0:T(8,128)S(1)}, f32[7,8,128]{2,1,0:T(8,128)S(1)}, u32[]{:S(2)}, u32[]{:S(2)}) collective-permute-start(f32[7,8,128]{2,1,0:T(8,128)S(1)} %get-tuple-element.13), channel_id=1, source_target_pairs={{0,1},{1,2},{2,3},{3,4},{4,5},{5,6},{6,7},{8,9},{9,10},{10,11},{11... | collective-permute-start | bytes 86024 | tf_op jit(solution)/shard_map/ppermute | solution.py:455
  10.4 6.3 %collective-permute-start.3 = (f32[13,16,128]{2,1,0:T(8,128)S(1)}, f32[13,16,128]{2,1,0:T(8,128)S(1)}, u32[]{:S(2)}, u32[]{:S(2)}) collective-permute-start(f32[13,16,128]{2,1,0:T(8,128)S(1)} %shard_map.78.wide), channel_id=1, source_target_pairs={{16,32},{48,64},{80,96},{112,128},{144,160},{176,192},{208,224},{2... | collective-permute-start | bytes 319496 | tf_op jit(solution)/shard_map/ppermute | solution.py:460
  11.0 7.7 %collective-permute-start.2 = (f32[13,16,128]{2,1,0:T(8,128)S(1)}, f32[13,16,128]{2,1,0:T(8,128)S(1)}, u32[]{:S(2)}, u32[]{:S(2)}) collective-permute-start(f32[13,16,128]{2,1,0:T(8,128)S(1)} %shard_map.78.wide), channel_id=1, source_target_pairs={{0,16},{32,48},{64,80},{96,112},{128,144},{160,176},{192,208},{224... | collective-permute-start | bytes 319496 | tf_op jit(solution)/shard_map/ppermute | solution.py:460
  18.7 14.8 %collective-permute-start.4 = (f32[2,13,16,128]{3,2,1,0:T(8,128)S(1)}, f32[2,13,16,128]{3,2,1,0:T(8,128)S(1)}, u32[]{:S(2)}, u32[]{:S(2)}) collective-permute-start(f32[2,13,16,128]{3,2,1,0:T(8,128)S(1)} %get-tuple-element.15), channel_id=1, source_target_pairs={{0,8},{8,0},{1,9},{9,1},{2,10},{10,2},{3,11},{11,3},{4,12},{12,4},... | collective-permute-start | bytes 638984 | tf_op jit(solution)/shard_map/ppermute | solution.py:518

commit v7 on v4

--- a/solution.py
+++ b/solution.py
@@ -498,7 +498,7 @@
             scalars=2,
         )(core, odd_chip, wide, first, second)
         taken = lax.ppermute(given, ("core",), [(0, 1), (1, 0)])
-        near, far = along * count_z, 2 * across
+        near, far = 2 * along, across * count_z
         basis, sums = call(
             krylov_body,
             (SDS((ITERS, 3, 3, ROWS, 128), F32), SDS((near, 128), F32)),
@@ -510,9 +510,9 @@
             ),
             flops=20000000,
         )(sides, taken, wide, table)
-        group = lax.all_to_all(sums.reshape(near, 1, 128), ("x", "z"), 0, 0)
+        group = lax.all_to_all(sums.reshape(near, 1, 128), ("x", "core"), 0, 0)
         partial = call(middle_body, SDS((far, 128), F32), 1)(group.reshape(near, 128))
-        everything = lax.all_to_all(partial.reshape(far, 1, 128), ("y", "core"), 0, 0)
+        everything = lax.all_to_all(partial.reshape(far, 1, 128), ("y", "z"), 0, 0)
         return tuple(
             call(final_body, (SDS((3, 2, 8, 128), F32), SDS((6, 2, 8, 128), F32)), 4)(
                 jnp.pad(everything.reshape(far, 128), ((0, -far % 8), (0, 0))), basis, own, table

time: 75.3 us -> 73.9 us (0.981)
  blocking collectives: 38.2 us -> 36.8 us
    all_to_all x2, blocking collectives: 38.2 us -> 36.8 us  [the longest x1 27 us: shards(): everything = lax.all_to_all(partial.reshape(far, 1, 128), ('y', 'z'), 0, 0)]
where the time goes in v7:
time: 73.9 us; the launch traced here: 73.6 us
  blocking collectives  36.8 us (50%)
  starting transfers between devices  27.7 us (37%)
  waiting for transfers between devices  4.23 us (6%)
  Pallas kernels  4.14 us (6%)
    all_to_all x1, blocking collectives, shards(): everything = lax.all_to_all(partial.reshape(far, 1, 128), ('y', 'z'), 0, 0)  27 us
    ppermute x1, starting transfers between devices, shards(): taken = lax.ppermute(given, ('core',), [(0, 1), (1, 0)])  13.8 us
    all_to_all x1, blocking collectives, shards(): group = lax.all_to_all(sums.reshape(near, 1, 128), ('x', 'core'), 0, 0)  9.81 us
    ppermute x2, starting transfers between devices, shifted(): return lax.ppermute(value, axes, pairs)  7.66 us
    ppermute x2, starting transfers between devices, swapped(): lax.ppermute(value, axes, [(i, i + 1) for i in lower] + [(i + 1, i) for i...  6.24 us
    ppermute x2, waiting for transfers between devices, swapped(): lax.ppermute(value, axes, [(i, i + 1) for i in lower] + [(i + 1, i) for i...  2.05 us
  transfers between devices with their start and end apart: 5, of which 3 were waited for; matrix products, arithmetic and copies ran while one was open for 0% of the time, Pallas kernels for 0%

profile of v7, /device:TPU:1, one launch (start us, length us, event | category | flops | bytes accessed | tf_op | source)
XLA Modules:
  0.0 73.6 jit_solution(17046721719861407128)
XLA Ops:
  0.6 0.9 %shard_map.77 = (f32[22,8,128]{2,1,0:T(8,128)S(1)}, f32[11,8,128]{2,1,0:T(8,128)S(1)}, f32[11,8,128]{2,1,0:T(8,128)S(1)}, f32[8,128]{1,0:T(8,128)S(1)}) custom-call(f32[6,8,128]{2,1,0:T(8,128)} %bitcast.18, f32[12,8,128]{2,1,0:T(8,128)} %bitcast.17, s32[2,8,128]{2,1,0:T(8,128)} %material.1, s32[2,8,128]{2,1,0:T(8,128)} %free.1, f32[3,16]{1,0:T(4,128)} %moduli.1, ...), custom_call_target="tpu_custom_call" | custom-call | flops 100000 | bytes 100000 | tf_op jit(solution)/shard_map/pallas_call | solution.py:464
  1.5 1.3 %collective-permute-start = (f32[11,8,128]{2,1,0:T(8,128)S(1)}, f32[11,8,128]{2,1,0:T(8,128)S(1)}, u32[]{:S(2)}, u32[]{:S(2)}) collective-permute-start(f32[11,8,128]{2,1,0:T(8,128)S(1)} %get-tuple-element.11), channel_id=1, source_target_pairs={{1,0},{2,1},{3,2},{4,3},{5,4},{6,5},{7,6},{9,8},{10,9},{11,10},{12... | collective-permute-start | bytes 135176 | tf_op jit(solution)/shard_map/ppermute | solution.py:444
  2.8 6.4 %collective-permute-start.1 = (f32[11,8,128]{2,1,0:T(8,128)S(1)}, f32[11,8,128]{2,1,0:T(8,128)S(1)}, u32[]{:S(2)}, u32[]{:S(2)}) collective-permute-start(f32[11,8,128]{2,1,0:T(8,128)S(1)} %get-tuple-element.12), channel_id=1, source_target_pairs={{0,1},{1,2},{2,3},{3,4},{4,5},{5,6},{6,7},{8,9},{9,10},{10,11},{11... | collective-permute-start | bytes 135176 | tf_op jit(solution)/shard_map/ppermute | solution.py:444
  9.2 0.0 collective-permute-done.above
  9.2 1.1 %collective-permute-done.1.below = f32[11,8,128]{2,1,0:T(8,128)S(1)} collective-permute-done((f32[11,8,128]{2,1,0:T(8,128)S(1)}, f32[11,8,128]{2,1,0:T(8,128)S(1)}, u32[]{:S(2)}, u32[]{:S(2)}) %collective-permute-start.1) | collective-permute-done | bytes 45088 | tf_op jit(solution)/shard_map/ppermute | solution.py:444
  10.3 0.2 shard_map.78.wide
  10.5 0.7 collective-permute-start.3
  11.2 5.6 %collective-permute-start.2 = (f32[13,16,128]{2,1,0:T(8,128)S(1)}, f32[13,16,128]{2,1,0:T(8,128)S(1)}, u32[]{:S(2)}, u32[]{:S(2)}) collective-permute-start(f32[13,16,128]{2,1,0:T(8,128)S(1)} %shard_map.78.wide), channel_id=1, source_target_pairs={{0,16},{32,48},{64,80},{96,112},{128,144},{160,176},{192,208},{224... | collective-permute-start | bytes 319496 | tf_op jit(solution)/shard_map/ppermute | solution.py:449
  16.8 0.0 collective-permute-done.3.second
  16.8 2.1 %collective-permute-done.2.first = f32[13,16,128]{2,1,0:T(8,128)S(1)} collective-permute-done((f32[13,16,128]{2,1,0:T(8,128)S(1)}, f32[13,16,128]{2,1,0:T(8,128)S(1)}, u32[]{:S(2)}, u32[]{:S(2)}) %collective-permute-start.2) | collective-permute-done | bytes 106528 | tf_op jit(solution)/shard_map/ppermute | solution.py:449
  18.9 13.8 %collective-permute-start.4 = (f32[2,13,16,128]{3,2,1,0:T(8,128)S(1)}, f32[2,13,16,128]{3,2,1,0:T(8,128)S(1)}, u32[]{:S(2)}, u32[]{:S(2)}) collective-permute-start(f32[2,13,16,128]{3,2,1,0:T(8,128)S(1)} %get-tuple-element.15), channel_id=1, source_target_pairs={{0,8},{8,0},{1,9},{9,1},{2,10},{10,2},{3,11},{11,3},{4,12},{12,4},... | collective-permute-start | bytes 638984 | tf_op jit(solution)/shard_map/ppermute | solution.py:500
  32.7 1.1 %collective-permute-done.4.rec = f32[2,13,16,128]{3,2,1,0:T(8,128)S(1)} collective-permute-done((f32[2,13,16,128]{3,2,1,0:T(8,128)S(1)}, f32[2,13,16,128]{3,2,1,0:T(8,128)S(1)}, u32[]{:S(2)}, u32[]{:S(2)}) %collective-permute-start.4) | collective-permute-done | bytes 213024 | tf_op jit(solution)/shard_map/ppermute | solution.py:500
  33.7 1.5 %shard_map.80 = (f32[4,3,3,16,128]{4,3,2,1,0:T(8,128)S(1)}, f32[16,128]{1,0:T(8,128)S(1)}) custom-call(f32[2,13,16,128]{3,2,1,0:T(8,128)S(1)} %get-tuple-element.14.sides, f32[2,13,16,128]{3,2,1,0:T(8,128)S(1)} %collective-permute-done.4.rec, f32[13,16,128]{2,1,0:T(8,128)S(1)} %shard_map.78.wide, f32[8,128]{1,0:T(8,128)S(1)} %get-tuple-element.13.table), custom_call_target="tpu_custom_call" | custom-call | flops 20000000 | bytes 100000 | tf_op jit(solution)/shard_map/pallas_call | solution.py:502
  35.2 9.8 %all_to_all.10 = f32[16,1,128]{2,1,0:T(1,128)S(1)} all-to-all(f32[16,1,128]{2,1,0:T(1,128)S(1)} %bitcast.16), channel_id=1, replica_groups=mesh['y'=8,'x'=8,'core'=2,'z'=8] {'x','core'}, dimensions={0} | all-to-all | bytes 16384 | tf_op jit(solution)/shard_map/all_to_all | solution.py:513
  45.0 0.2 shard_map.81
  45.2 27.0 %all_to_all.11 = f32[64,1,128]{2,1,0:T(1,128)S(1)} all-to-all(f32[64,1,128]{2,1,0:T(1,128)S(1)} %bitcast.14), channel_id=1, replica_groups=mesh['y'=8,'x'=8,'core'=2,'z'=8] {'y','z'}, dimensions={0} | all-to-all | bytes 65536 | tf_op jit(solution)/shard_map/all_to_all | solution.py:515
  72.2 1.4 %shard_map.82 = (f32[3,2,8,128]{3,2,1,0:T(8,128)}, f32[6,2,8,128]{3,2,1,0:T(8,128)}) custom-call(f32[64,128]{1,0:T(8,128)S(1)} %bitcast.13, f32[4,3,3,16,128]{4,3,2,1,0:T(8,128)S(1)} %get-tuple-element.17.basis, f32[22,8,128]{2,1,0:T(8,128)S(1)} %get-tuple-element.10.own, f32[8,128]{1,0:T(8,128)S(1)} %get-tuple-element.13.table), custom_call_target="tpu_custom_call" | custom-call | flops 100000 | bytes 100000 | tf_op jit(solution)/shard_map/pallas_call | solution.py:517
  (1 shorter events, 0.0 us)
Async XLA Ops:
  1.5 7.7 %collective-permute-start = (f32[11,8,128]{2,1,0:T(8,128)S(1)}, f32[11,8,128]{2,1,0:T(8,128)S(1)}, u32[]{:S(2)}, u32[]{:S(2)}) collective-permute-start(f32[11,8,128]{2,1,0:T(8,128)S(1)} %get-tuple-element.11), channel_id=1, source_target_pairs={{1,0},{2,1},{3,2},{4,3},{5,4},{6,5},{7,6},{9,8},{10,9},{11,10},{12... | collective-permute-start | bytes 135176 | tf_op jit(solution)/shard_map/ppermute | solution.py:444
  2.8 7.5 %collective-permute-start.1 = (f32[11,8,128]{2,1,0:T(8,128)S(1)}, f32[11,8,128]{2,1,0:T(8,128)S(1)}, u32[]{:S(2)}, u32[]{:S(2)}) collective-permute-start(f32[11,8,128]{2,1,0:T(8,128)S(1)} %get-tuple-element.12), channel_id=1, source_target_pairs={{0,1},{1,2},{2,3},{3,4},{4,5},{5,6},{6,7},{8,9},{9,10},{10,11},{11... | collective-permute-start | bytes 135176 | tf_op jit(solution)/shard_map/ppermute | solution.py:444
  10.5 6.3 %collective-permute-start.3 = (f32[13,16,128]{2,1,0:T(8,128)S(1)}, f32[13,16,128]{2,1,0:T(8,128)S(1)}, u32[]{:S(2)}, u32[]{:S(2)}) collective-permute-start(f32[13,16,128]{2,1,0:T(8,128)S(1)} %shard_map.78.wide), channel_id=1, source_target_pairs={{16,32},{48,64},{80,96},{112,128},{144,160},{176,192},{208,224},{2... | collective-permute-start | bytes 319496 | tf_op jit(solution)/shard_map/ppermute | solution.py:449
  11.2 7.7 %collective-permute-start.2 = (f32[13,16,128]{2,1,0:T(8,128)S(1)}, f32[13,16,128]{2,1,0:T(8,128)S(1)}, u32[]{:S(2)}, u32[]{:S(2)}) collective-permute-start(f32[13,16,128]{2,1,0:T(8,128)S(1)} %shard_map.78.wide), channel_id=1, source_target_pairs={{0,16},{32,48},{64,80},{96,112},{128,144},{160,176},{192,208},{224... | collective-permute-start | bytes 319496 | tf_op jit(solution)/shard_map/ppermute | solution.py:449
  18.9 14.8 %collective-permute-start.4 = (f32[2,13,16,128]{3,2,1,0:T(8,128)S(1)}, f32[2,13,16,128]{3,2,1,0:T(8,128)S(1)}, u32[]{:S(2)}, u32[]{:S(2)}) collective-permute-start(f32[2,13,16,128]{3,2,1,0:T(8,128)S(1)} %get-tuple-element.15), channel_id=1, source_target_pairs={{0,8},{8,0},{1,9},{9,1},{2,10},{10,2},{3,11},{11,3},{4,12},{12,4},... | collective-permute-start | bytes 638984 | tf_op jit(solution)/shard_map/ppermute | solution.py:500
